TPU v7x, 512 devices: a whole 4x8x8 slice. The times are simulated.
512 devices in a mesh: dp: 8 (over x, core), expert: 64 (over z, y).
Axes of the slice: x: 4, y: 8, z: 8, core: 2. Of those that a mesh axis runs over, the one named last changes fastest.
Arguments:
- tokens: bfloat16 [65536, 1024], P(('dp', 'expert')), may hold values from -6 to 6
- routes: int32 [65536, 6], P(('dp', 'expert')), may hold values from 0 to 63, all different within a row; in each aligned block of 128 rows (0 to 127, 128 to 255, ...) at most 24 rows name the same one
- route_weights: float32 [65536, 6], P(('dp', 'expert')), may hold values from 0.1 to 1
- gate_weight: bfloat16 [64, 1024, 512], P('expert'), may hold values from -0.1875 to 0.1875
- up_weight: bfloat16 [64, 1024, 512], P('expert'), may hold values from -0.1875 to 0.1875
- down_weight: bfloat16 [64, 512, 1024], P('expert'), may hold values from -0.25 to 0.25
- cotangent: bfloat16 [65536, 1024], P(('dp', 'expert')), may hold values from -3 to 3
Outputs:
- mixed_latent: bfloat16 [65536, 1024], P(('dp', 'expert'))
- latent_grad: bfloat16 [65536, 1024], P(('dp', 'expert'))
- gate_grad: float32 [64, 1024, 512], P('expert', 'dp')
- up_grad: float32 [64, 1024, 512], P('expert', 'dp')
- down_grad: float32 [64, 512, 1024], P('expert', None, 'dp')
Inputs may be any that keep to these rules, and one draw needn't show every extreme that they name: `routes`: each row names 6 different experts. In each aligned block of 128 rows (the rows of one device) no expert is named by more than 24 rows, and some expert is named by exactly 24 rows in some block.
All inputs are finite; a program needn't handle non-finite values.
Results may differ from a plain program's by a relative error of at most 0.015.
Values may be sent and summed in bfloat16 or wider, within the bound.
No kernel may reach another device: no remote copies, remote signals or barrier semaphores. Data moves between devices by JAX's collectives and lax.ppermute only.
A program may use at most 64 MiB of HBM per device.

v0:
```python
import jax
import jax.numpy as jnp
from jax import lax
from jax.sharding import PartitionSpec as P


def slot_plan(route_rows, experts, capacity):
    flat_routes = route_rows.reshape(-1)
    one_hot = (flat_routes[:, None] == jnp.arange(experts, dtype=jnp.int32)[None, :]).astype(
        jnp.int32
    )
    earlier = jnp.cumsum(one_hot, axis=0) - one_hot
    slot_rank = jnp.sum(earlier * one_hot, axis=1)
    kept_mask = slot_rank < capacity
    slot_index = jnp.where(kept_mask, flat_routes * capacity + slot_rank, experts * capacity)
    return (kept_mask, slot_index)


def pack_rows(row_values, slot_index, experts, capacity):
    latent_width = row_values.shape[1]
    buffer = jnp.zeros((experts * capacity + 1, latent_width), row_values.dtype)
    buffer = buffer.at[slot_index].set(row_values)
    return buffer[:-1].reshape(experts, capacity, latent_width)


def unpack_rows(buffer, slot_index, top_count):
    latent_width = buffer.shape[-1]
    padded = jnp.concatenate(
        [buffer.reshape(-1, latent_width), jnp.zeros((1, latent_width), buffer.dtype)], axis=0
    )
    return padded[slot_index].reshape(-1, top_count, latent_width)


def expert_forward(inputs, gate_matrix, up_matrix, down_matrix):
    gate_pre = jnp.dot(inputs, gate_matrix, preferred_element_type=jnp.float32)
    up_pre = jnp.dot(inputs, up_matrix, preferred_element_type=jnp.float32)
    hidden = (jax.nn.silu(gate_pre) * up_pre).astype(jnp.bfloat16)
    outputs = jnp.dot(hidden, down_matrix, preferred_element_type=jnp.float32).astype(jnp.bfloat16)
    return (outputs, gate_pre, up_pre, hidden)


def expert_backward(out_grads, gate_pre, up_pre, gate_matrix, up_matrix, down_matrix):
    contract_last = (((1,), (1,)), ((), ()))
    hidden_grad = lax.dot_general(
        out_grads, down_matrix, contract_last, preferred_element_type=jnp.float32
    )
    sigmoid_gate = jax.nn.sigmoid(gate_pre)
    up_grad_pre = (hidden_grad * gate_pre * sigmoid_gate).astype(jnp.bfloat16)
    gate_grad_pre = (
        hidden_grad * up_pre * sigmoid_gate * (1.0 + gate_pre * (1.0 - sigmoid_gate))
    ).astype(jnp.bfloat16)
    input_grads = lax.dot_general(
        gate_grad_pre, gate_matrix, contract_last, preferred_element_type=jnp.float32
    )
    input_grads = input_grads + lax.dot_general(
        up_grad_pre, up_matrix, contract_last, preferred_element_type=jnp.float32
    )
    return (input_grads.astype(jnp.bfloat16), gate_grad_pre, up_grad_pre)


def shards(tokens, routes, route_weights, gate_weight, up_weight, down_weight, cotangent):
    token_count, latent_width = tokens.shape
    top_count = routes.shape[1]
    experts = lax.axis_size("expert")
    capacity = token_count * top_count // experts
    kept_mask, slot_index = slot_plan(routes, experts, capacity)
    kept_weights = route_weights * kept_mask.reshape(token_count, top_count).astype(jnp.float32)
    send_tokens = pack_rows(jnp.repeat(tokens, top_count, axis=0), slot_index, experts, capacity)
    grad_rows = (kept_weights[:, :, None] * cotangent[:, None, :].astype(jnp.float32)).astype(
        jnp.bfloat16
    )
    send_grads = pack_rows(
        grad_rows.reshape(token_count * top_count, latent_width), slot_index, experts, capacity
    )
    gate_matrix = gate_weight[0]
    up_matrix = up_weight[0]
    down_matrix = down_weight[0]
    inbox_tokens = lax.all_to_all(send_tokens, "expert", split_axis=0, concat_axis=0, tiled=True)
    inputs = inbox_tokens.reshape(-1, latent_width)
    outputs, gate_pre, up_pre, hidden = expert_forward(inputs, gate_matrix, up_matrix, down_matrix)
    returned_outputs = lax.all_to_all(
        outputs.reshape(experts, capacity, latent_width),
        "expert",
        split_axis=0,
        concat_axis=0,
        tiled=True,
    )
    inbox_grads = lax.all_to_all(send_grads, "expert", split_axis=0, concat_axis=0, tiled=True)
    out_grads = inbox_grads.reshape(-1, latent_width)
    input_grads, gate_grad_pre, up_grad_pre = expert_backward(
        out_grads, gate_pre, up_pre, gate_matrix, up_matrix, down_matrix
    )
    returned_grads = lax.all_to_all(
        input_grads.reshape(experts, capacity, latent_width),
        "expert",
        split_axis=0,
        concat_axis=0,
        tiled=True,
    )
    mixed_latent = jnp.sum(
        unpack_rows(returned_outputs, slot_index, top_count).astype(jnp.float32)
        * kept_weights[:, :, None],
        axis=1,
    ).astype(jnp.bfloat16)
    latent_grad = jnp.sum(
        unpack_rows(returned_grads, slot_index, top_count).astype(jnp.float32), axis=1
    ).astype(jnp.bfloat16)
    contract_rows = (((0,), (0,)), ((), ()))
    pair_grads = jnp.concatenate([gate_grad_pre, up_grad_pre], axis=1)
    ffn_width = hidden.shape[1]
    window = inputs
    pair_share = lax.psum_scatter(
        lax.dot_general(
            window, pair_grads, contract_rows, preferred_element_type=jnp.float32
        ).astype(jnp.bfloat16),
        "dp",
        scatter_dimension=0,
        tiled=True,
    ).astype(jnp.float32)
    window = out_grads
    down_share = lax.psum_scatter(
        lax.dot_general(window, hidden, contract_rows, preferred_element_type=jnp.float32).astype(
            jnp.bfloat16
        ),
        "dp",
        scatter_dimension=0,
        tiled=True,
    ).astype(jnp.float32)
    gate_grad = pair_share[:, :ffn_width][None]
    up_grad = pair_share[:, ffn_width:][None]
    down_grad = down_share.T[None]
    return (mixed_latent, latent_grad, gate_grad, up_grad, down_grad)


def solution(mesh):
    placed = (
        P(("dp", "expert"), None),
        P(("dp", "expert"), None),
        P(("dp", "expert"), None),
        P("expert", None, None),
        P("expert", None, None),
        P("expert", None, None),
        P(("dp", "expert"), None),
    )
    return jax.shard_map(
        shards,
        mesh=mesh,
        in_specs=placed,
        out_specs=(
            P(("dp", "expert"), None),
            P(("dp", "expert"), None),
            P("expert", "dp", None),
            P("expert", "dp", None),
            P("expert", None, "dp"),
        ),
        check_vma=False,
    )
```

profile of v0, /device:TPU:2, one launch (start us, length us, event | category | flops | bytes accessed | tf_op | source)
XLA Modules:
  0.0 306.7 jit_solution(10751837814814026483)
XLA Ops:
  9.1 1.8 reduce-window.6
  14.3 6.8 %scatter_custom_fusion = bf16[769,1024]{1,0:T(8,128)(2,1)S(1)} fusion(s32[768]{0:T(1024)S(1)} %fusion.22, bf16[768,1024]{1,0:T(8,128)(2,1)} %reshape.138, bf16[]{:T(256)} %constant.7.clone.1), kind=kCustom, calls=%fused_computation.30 | custom fusion | bytes 1575424 | tf_op jit(solution)/shard_map/scatter | solution.py:22
  22.4 3.6 %reshape.107 = bf16[64,12,1024]{2,1,0:T(8,128)(2,1)} reshape(bf16[768,1024]{1,0:T(8,128)(2,1)} %slice.29) | data formatting | bytes 3145728 | tf_op jit(solution)/shard_map/reshape | solution.py:23
  26.0 16.7 %all-to-all-start = ((bf16[64,12,1024]{2,1,0:T(8,128)(2,1)}), bf16[64,12,1024]{2,1,0:T(8,128)(2,1)S(1)}, u32[]{:S(2)}, u32[]{:S(2)}) async-start(bf16[64,12,1024]{2,1,0:T(8,128)(2,1)} %reshape.107), calls=%async_computation | async-start | bytes 4194304 | tf_op jit(solution)/shard_map/all_to_all | solution.py:78
  43.2 2.5 mul.80
  45.8 4.7 %mul.81 = f32[768,1024]{1,0:T(8,128)} reshape(f32[128,6,1024]{2,1,0:T(8,128)} %mul.80) | data formatting | bytes 6291456 | tf_op jit(solution)/shard_map/mul | solution.py:69
  50.5 11.0 %scatter_custom_fusion.1 = bf16[769,1024]{1,0:T(8,128)(2,1)} fusion(s32[768]{0:T(1024)S(1)} %copy-done.10, f32[768,1024]{1,0:T(8,128)} %mul.81, f32[768]{0:T(1024)S(1)} %mul.78, bf16[]{:T(256)} %constant.7.clone.1), kind=kCustom, calls=%fused_computation.9 | custom fusion | flops 1572864 | bytes 4724738 | tf_op jit(solution)/shard_map/scatter | solution.py:22
  61.5 2.7 slice.30
  64.2 3.6 %reshape.111 = bf16[64,12,1024]{2,1,0:T(8,128)(2,1)} reshape(bf16[768,1024]{1,0:T(8,128)(2,1)} %slice.30) | data formatting | bytes 3145728 | tf_op jit(solution)/shard_map/reshape | solution.py:23
  67.8 27.4 %all-to-all-done = bf16[64,12,1024]{2,1,0:T(8,128)(2,1)S(1)} async-done(((bf16[64,12,1024]{2,1,0:T(8,128)(2,1)}), bf16[64,12,1024]{2,1,0:T(8,128)(2,1)S(1)}, u32[]{:S(2)}, u32[]{:S(2)}) %all-to-all-start) | async-done | bytes 1572896 | tf_op jit(solution)/shard_map/all_to_all | solution.py:78
  95.1 9.5 %all-to-all-start.2 = ((bf16[64,12,1024]{2,1,0:T(8,128)(2,1)}), bf16[64,12,1024]{2,1,0:T(8,128)(2,1)}, u32[]{:S(2)}, u32[]{:S(2)}) async-start(bf16[64,12,1024]{2,1,0:T(8,128)(2,1)} %reshape.111), calls=%async_computation.2 | async-start | bytes 4194304 | tf_op jit(solution)/shard_map/all_to_all | solution.py:88
  106.0 4.1 %fusion.13 = f32[768,512]{0,1:T(8,128)} fusion(bf16[768,1024]{1,0:T(8,128)(2,1)} %reshape.108, bf16[1,1024,512]{2,1,0:T(8,128)(2,1)} %param.10), kind=kOutput, calls=%fused_computation.27 | convolution fusion | flops 805306368 | bytes 4194304 | tf_op jit(solution)/shard_map/dot_general | solution.py:35
  110.1 2.3 fusion.9
  112.4 43.7 %all-to-all-done.2 = bf16[64,12,1024]{2,1,0:T(8,128)(2,1)} async-done(((bf16[64,12,1024]{2,1,0:T(8,128)(2,1)}), bf16[64,12,1024]{2,1,0:T(8,128)(2,1)}, u32[]{:S(2)}, u32[]{:S(2)}) %all-to-all-start.2) | async-done | bytes 1572896 | tf_op jit(solution)/shard_map/all_to_all | solution.py:88
  156.1 2.5 reshape.112
  158.7 4.9 %multiply_convert_fusion.2 = (bf16[768,512]{0,1:T(8,128)(2,1)S(1)}, bf16[768,512]{0,1:T(8,128)(2,1)S(1)}, bf16[768,512]{0,1:T(8,128)(2,1)}) fusion(f32[768,512]{0,1:T(8,128)} %fusion.13, f32[768,512]{0,1:T(8,128)} %fusion.9, bf16[768,1024]{1,0:T(8,128)(2,1)S(1)} %reshape.112, bf16[1,512,1024]{2,1,0:T(8,128)(2,1)S(1)} %copy-done), kind=kOutput, calls=%fused_computation.13 | convolution fusion | flops 811597824 | bytes 8126464 | tf_op jit(solution)/shard_map/dot_general | solution.py:44
  168.0 6.5 %all-to-all-start.3 = ((bf16[64,12,1024]{2,1,0:T(8,128)(2,1)}), bf16[64,12,1024]{2,1,0:T(8,128)(2,1)S(1)}, u32[]{:S(2)}, u32[]{:S(2)}) async-start(bf16[64,12,1024]{2,1,0:T(8,128)(2,1)} %reshape.113), calls=%async_computation.3 | async-start | bytes 4194304 | tf_op jit(solution)/shard_map/all_to_all | solution.py:93
  174.5 3.6 %convolution_convert_fusion.2 = bf16[1024,512]{1,0:T(8,128)(2,1)} fusion(bf16[768,1024]{1,0:T(8,128)(2,1)} %copy-done.3, bf16[768,512]{0,1:T(8,128)(2,1)} %get-tuple-element.17), kind=kOutput, calls=%fused_computation.18 | convolution fusion | flops 805830656 | bytes 3407872 | tf_op jit(solution)/shard_map/dot_general | solution.py:122
  178.2 5.0 %convolution_convert_fusion = bf16[1024,1024]{1,0:T(8,128)(2,1)} fusion(bf16[768,1024]{1,0:T(8,128)(2,1)} %reshape.108, bf16[768,512]{0,1:T(8,128)(2,1)} %copy-done.7, bf16[768,512]{0,1:T(8,128)(2,1)} %copy-done.1), kind=kOutput, calls=%fused_computation.7 | convolution fusion | flops 1614807040 | bytes 5242880 | tf_op jit(solution)/shard_map/dot_general | solution.py:113
  183.3 3.4 %convolution_convert_fusion.1 = bf16[768,1024]{1,0:T(8,128)(2,1)} fusion(bf16[768,512]{0,1:T(8,128)(2,1)} %get-tuple-element.17, bf16[1,512,1024]{2,1,0:T(8,128)(2,1)S(1)} %copy-done), kind=kOutput, calls=%fused_computation.8 | convolution fusion | flops 806092800 | bytes 3407872 | tf_op jit(solution)/shard_map/dot_general | solution.py:38
  186.6 3.6 %reshape.109 = bf16[64,12,1024]{2,1,0:T(8,128)(2,1)} reshape(bf16[768,1024]{1,0:T(8,128)(2,1)} %convolution_convert_fusion.1) | data formatting | bytes 3145728 | tf_op jit(solution)/shard_map/reshape | solution.py:82
  190.2 34.8 %all-to-all-done.3 = bf16[64,12,1024]{2,1,0:T(8,128)(2,1)S(1)} async-done(((bf16[64,12,1024]{2,1,0:T(8,128)(2,1)}), bf16[64,12,1024]{2,1,0:T(8,128)(2,1)S(1)}, u32[]{:S(2)}, u32[]{:S(2)}) %all-to-all-start.3) | async-done | bytes 1572896 | tf_op jit(solution)/shard_map/all_to_all | solution.py:93
  225.0 6.8 %all-to-all-start.1 = ((bf16[64,12,1024]{2,1,0:T(8,128)(2,1)}), bf16[64,12,1024]{2,1,0:T(8,128)(2,1)}, u32[]{:S(2)}, u32[]{:S(2)}) async-start(bf16[64,12,1024]{2,1,0:T(8,128)(2,1)} %reshape.109), calls=%async_computation.1 | async-start | bytes 4194304 | tf_op jit(solution)/shard_map/all_to_all | solution.py:81
  235.0 1.6 concatenate.10
  236.6 3.6 %gather_fusion.1 = bf16[768,1024]{1,0:T(8,128)(2,1)} fusion(bf16[769,1024]{1,0:T(8,128)(2,1)S(1)} %concatenate.10, s32[1024]{0:T(1024)S(1)} %pad_clamp_fusion), kind=kCustom, calls=%fused_computation.1 | custom fusion | bytes 3148800 | tf_op jit(solution)/shard_map/gather | solution.py:31
  240.2 2.5 reshape.115
  242.7 2.2 reduce_sum.35
  244.9 36.3 %all-to-all-done.1 = bf16[64,12,1024]{2,1,0:T(8,128)(2,1)} async-done(((bf16[64,12,1024]{2,1,0:T(8,128)(2,1)}), bf16[64,12,1024]{2,1,0:T(8,128)(2,1)}, u32[]{:S(2)}, u32[]{:S(2)}) %all-to-all-start.1) | async-done | bytes 1572896 | tf_op jit(solution)/shard_map/all_to_all | solution.py:81
  281.1 3.6 %reshape.110 = bf16[768,1024]{1,0:T(8,128)(2,1)} reshape(bf16[64,12,1024]{2,1,0:T(8,128)(2,1)} %all-to-all-done.1) | data formatting | bytes 3145728 | tf_op jit(solution)/shard_map/reshape | solution.py:29
  286.3 3.6 %gather_fusion = bf16[768,1024]{1,0:T(8,128)(2,1)} fusion(bf16[769,1024]{1,0:T(8,128)(2,1)S(1)} %concatenate.9, s32[1024]{0:T(1024)S(1)} %pad_clamp_fusion), kind=kCustom, calls=%fused_computation | custom fusion | bytes 3148800 | tf_op jit(solution)/shard_map/gather | solution.py:31
  289.9 3.9 %reshape.116 = f32[128,6,1024]{2,1,0:T(8,128)} reshape(bf16[768,1024]{1,0:T(8,128)(2,1)} %gather_fusion) | data formatting | bytes 4718592 | tf_op jit(solution)/shard_map/convert_element_type | solution.py:101
  293.8 4.3 %multiply_reduce_fusion = bf16[128,1024]{1,0:T(8,128)(2,1)} fusion(f32[128,6,1024]{2,1,0:T(8,128)} %reshape.116, f32[128,6]{1,0:T(8,128)S(1)} %broadcast_select_fusion), kind=kLoop, calls=%fused_computation.4 | loop fusion | flops 1441792 | bytes 3410944 | tf_op jit(solution)/shard_map/reduce_sum | solution.py:100
  (60 shorter events, 19.4 us)
Async XLA Ops:
  7.2 151.5 %copy-start = (bf16[1,512,1024]{2,1,0:T(8,128)(2,1)S(1)}, bf16[1,512,1024]{2,1,0:T(8,128)(2,1)}, u32[]{:S(2)}) copy-start(bf16[1,512,1024]{2,1,0:T(8,128)(2,1)} %param.12) | copy-start | bytes 3145732
  14.3 8.1 %copy-start.9 = (s32[768]{0:T(1024)}, s32[768]{0:T(1024)S(1)}, u32[]{:S(2)}) copy-start(s32[768]{0:T(1024)S(1)} %fusion.22) | copy-start | bytes 9220
  26.0 16.9 %copy-start.11 = (f32[128,6]{0,1:T(8,128)S(1)}, f32[128,6]{0,1:T(8,128)}, u32[]{:S(2)}) copy-start(f32[128,6]{0,1:T(8,128)} %param.9) | copy-start | bytes 9220
  26.0 17.2 %copy-start.8 = (bf16[128,1024]{1,0:T(8,128)(2,1)S(1)}, bf16[128,1024]{1,0:T(8,128)(2,1)}, u32[]{:S(2)}) copy-start(bf16[128,1024]{1,0:T(8,128)(2,1)} %param.13) | copy-start | bytes 786436
  26.0 69.1 %all-to-all-start = ((bf16[64,12,1024]{2,1,0:T(8,128)(2,1)}), bf16[64,12,1024]{2,1,0:T(8,128)(2,1)S(1)}, u32[]{:S(2)}, u32[]{:S(2)}) async-start(bf16[64,12,1024]{2,1,0:T(8,128)(2,1)} %reshape.107), calls=%async_computation | async-start | bytes 4194304 | tf_op jit(solution)/shard_map/all_to_all | solution.py:78
  45.8 4.8 %copy-start.10 = (s32[768]{0:T(1024)S(1)}, s32[768]{0:T(1024)}, u32[]{:S(2)}) copy-start(s32[768]{0:T(1024)} %copy-done.9) | copy-start | bytes 9220
  95.1 61.0 %all-to-all-start.2 = ((bf16[64,12,1024]{2,1,0:T(8,128)(2,1)}), bf16[64,12,1024]{2,1,0:T(8,128)(2,1)}, u32[]{:S(2)}, u32[]{:S(2)}) async-start(bf16[64,12,1024]{2,1,0:T(8,128)(2,1)} %reshape.111), calls=%async_computation.2 | async-start | bytes 4194304 | tf_op jit(solution)/shard_map/all_to_all | solution.py:88
  106.0 4.1 %copy-start.2 = (bf16[768,1024]{1,0:T(8,128)(2,1)S(1)}, bf16[768,1024]{1,0:T(8,128)(2,1)}, u32[]{:S(2)}) copy-start(bf16[768,1024]{1,0:T(8,128)(2,1)} %reshape.108) | copy-start | bytes 4718596
  106.0 4.1 %copy-start.4 = (bf16[1,1024,512]{2,1,0:T(8,128)(2,1)S(1)}, bf16[1,1024,512]{2,1,0:T(8,128)(2,1)}, u32[]{:S(2)}) copy-start(bf16[1,1024,512]{2,1,0:T(8,128)(2,1)} %param.11) | copy-start | bytes 3145732
  158.6 4.9 %copy-start.3 = (bf16[768,1024]{1,0:T(8,128)(2,1)}, bf16[768,1024]{1,0:T(8,128)(2,1)S(1)}, u32[]{:S(2)}) copy-start(bf16[768,1024]{1,0:T(8,128)(2,1)S(1)} %reshape.112) | copy-start | bytes 4718596
  158.7 4.9 %copy-start.6 = (bf16[1,1024,512]{2,1,0:T(8,128)(2,1)S(1)}, bf16[1,1024,512]{2,1,0:T(8,128)(2,1)}, u32[]{:S(2)}) copy-start(bf16[1,1024,512]{2,1,0:T(8,128)(2,1)} %param.10) | copy-start | bytes 3145732
  163.6 1.1 copy-start.1
  163.6 1.2 copy-start.7
  163.6 1.8 copy-start.5
  168.0 57.1 %all-to-all-start.3 = ((bf16[64,12,1024]{2,1,0:T(8,128)(2,1)}), bf16[64,12,1024]{2,1,0:T(8,128)(2,1)S(1)}, u32[]{:S(2)}, u32[]{:S(2)}) async-start(bf16[64,12,1024]{2,1,0:T(8,128)(2,1)} %reshape.113), calls=%async_computation.3 | async-start | bytes 4194304 | tf_op jit(solution)/shard_map/all_to_all | solution.py:93
  174.5 57.4 %reduce-scatter.5.cloned.1.call-start = ((), (), s32[]{:S(2)}) async-start(), calls=%async_computation.7 | async-start | bytes 1179648 | tf_op jit(solution)/shard_map/reduce_scatter | solution.py:121
  178.1 119.9 %reduce-scatter.3.cloned.1.call-start = ((), (), s32[]{:S(2)}) async-start(), calls=%async_computation.6 | async-start | bytes 2359296 | tf_op jit(solution)/shard_map/reduce_scatter | solution.py:112
  225.0 56.1 %all-to-all-start.1 = ((bf16[64,12,1024]{2,1,0:T(8,128)(2,1)}), bf16[64,12,1024]{2,1,0:T(8,128)(2,1)}, u32[]{:S(2)}, u32[]{:S(2)}) async-start(bf16[64,12,1024]{2,1,0:T(8,128)(2,1)} %reshape.109), calls=%async_computation.1 | async-start | bytes 4194304 | tf_op jit(solution)/shard_map/all_to_all | solution.py:81
Sparse Core Ops, SparseCore 0:
  178.3 35.2 reduce-scatter.4
  216.4 38.5 reduce-scatter.2
where the time goes:
time: 308 us; the launch traced here: 307 us
  waiting for transfers between devices  142 us (46%)
  local copies, waits for them, and re-layouts  63.1 us (20%)
  starting transfers between devices  39.6 us (13%)
  matrix products  25.4 us (8%)
  other arithmetic  22.1 us (7%)
  between operations  14.3 us (5%)
    all_to_all x1, waiting for transfers between devices, shards(): lax.all_to_all(send_grads, 'expert', split_axis=0, concat_axis=0, tiled=T...  43.7 us
    all_to_all x1, waiting for transfers between devices, shards(): lax.all_to_all(outputs.reshape(experts, capacity, latent_width), 'expert'...  36.3 us
    all_to_all x1, waiting for transfers between devices, shards(): lax.all_to_all(input_grads.reshape(experts, capacity, latent_width), 'exp...  34.8 us
    all_to_all x1, waiting for transfers between devices, shards(): lax.all_to_all(send_tokens, 'expert', split_axis=0, concat_axis=0, tiled=...  27.4 us
    all_to_all x1, starting transfers between devices, shards(): lax.all_to_all(send_tokens, 'expert', split_axis=0, concat_axis=0, tiled=...  16.7 us
    scatter x1, other arithmetic, pack_rows(): buffer = buffer.at[slot_index].set(row_values)  11 us
    all_to_all x1, starting transfers between devices, shards(): lax.all_to_all(send_grads, 'expert', split_axis=0, concat_axis=0, tiled=T...  9.54 us
    mul x2, local copies, waits for them, and re-layouts, shards(): kept_weights[:, :, None] * cotangent[:, None, :].astype(jnp.float32)  7.29 us
  transfers between devices with their start and end apart: 6, of which 4 were waited for; matrix products, arithmetic and copies ran while one was open for 26% of the time, Pallas kernels for 0%

commit v1 on v0

v1 whole, which is shorter than its diff:
```python
import jax
import jax.numpy as jnp
from jax import lax
from jax.experimental import pallas as pl
from jax.experimental.pallas import tpu as pltpu
from jax.sharding import PartitionSpec as P

INTERPRET = False
F32 = jnp.float32
BF16 = jnp.bfloat16
NT = (((1,), (1,)), ((), ()))


def chunk_slot(row):
    slot = jnp.where(row < 12, row, jnp.where(row < 16, row - 4, row - 16))
    return slot.astype(F32), row >= 12


def route_tables(routes, weights, experts):
    top_count, token_count = routes.shape
    expert = lax.broadcasted_iota(jnp.int32, (experts, token_count), 0)
    named = jnp.zeros((experts, token_count), F32)
    weight = jnp.zeros((experts, token_count), F32)
    for k in range(top_count):
        same = routes[k : k + 1, :] == expert
        named = jnp.where(same, 1.0, named)
        weight = jnp.where(same, weights[k : k + 1, :], weight)
    earlier = lax.broadcasted_iota(jnp.int32, (token_count, token_count), 0)
    later = lax.broadcasted_iota(jnp.int32, (token_count, token_count), 1)
    before = jnp.where(earlier < later, 1.0, 0.0).astype(BF16)
    rank = jnp.dot(named.astype(BF16), before, preferred_element_type=F32)
    return jnp.where(named > 0.0, rank, -1.0), weight


def pack_kernel(experts, chunk, routes_ref, weights_ref, tokens_ref, cot_ref, send_ref, pick_ref, scale_ref):
    token_count = tokens_ref.shape[0]

    @pl.when(pl.program_id(0) == 0)
    def _():
        rank, weight = route_tables(routes_ref[...], weights_ref[...], experts)
        full = (experts, chunk, token_count)
        row = lax.broadcasted_iota(jnp.int32, full, 1)
        slot, backward = chunk_slot(row)
        hit = jnp.broadcast_to(rank[:, None, :], full) == slot
        one = jnp.where(hit, 1.0, 0.0)
        pick_ref[:, :token_count] = (
            jnp.where(backward, 0.0, one).reshape(experts * chunk, token_count).astype(BF16)
        )
        pick_ref[:, token_count:] = (
            jnp.where(backward, one, 0.0).reshape(experts * chunk, token_count).astype(BF16)
        )
        chosen = jnp.where(hit, jnp.broadcast_to(weight[:, None, :], full), 0.0)
        scale = jnp.where(backward, jnp.sum(chosen, axis=2, keepdims=True), 1.0)
        scale_ref[...] = scale.reshape(experts * chunk, token_count)

    rows = jnp.concatenate([tokens_ref[...], cot_ref[...]], axis=0)
    picked = jnp.dot(pick_ref[...], rows, preferred_element_type=F32)
    width = picked.shape[1]
    scale = scale_ref[...]
    for at in range(0, width, token_count):
        send_ref[:, at : at + token_count] = (picked[:, at : at + token_count] * scale).astype(BF16)


def pack(tokens, cotangent, routes, weights, experts, chunk):
    token_count, width = tokens.shape
    block = 256
    small = pl.BlockSpec(routes.shape, lambda j: (0, 0))
    wide = pl.BlockSpec((token_count, block), lambda j: (0, j))
    rows = experts * chunk
    return pl.pallas_call(
        lambda *refs: pack_kernel(experts, chunk, *refs),
        grid=(width // block,),
        in_specs=[small, small, wide, wide],
        out_specs=pl.BlockSpec((rows, block), lambda j: (0, j)),
        out_shape=jax.ShapeDtypeStruct((rows, width), BF16),
        scratch_shapes=[pltpu.VMEM((rows, 2 * token_count), BF16), pltpu.VMEM((rows, token_count), F32)],
        compiler_params=pltpu.CompilerParams(vmem_limit_bytes=32 * 1024 * 1024),
        cost_estimate=pl.CostEstimate(
            flops=4 * rows * token_count * width, bytes_accessed=2 * (rows + 2 * token_count) * width, transcendentals=0
        ),
        interpret=INTERPRET,
        name="pack",
    )(routes, weights, tokens, cotangent)


def plan_kernel(experts, chunk, routes_ref, weights_ref, plan_ref):
    token_count = routes_ref.shape[1]
    rank, weight = route_tables(routes_ref[...], weights_ref[...], 128)
    rank, weight = rank.T[:, :experts], weight.T[:, :experts]
    rows = experts * chunk
    owner = lax.broadcasted_iota(jnp.int32, (experts, rows), 0) * chunk
    place = lax.broadcasted_iota(jnp.int32, (experts, rows), 1) - owner
    spread = jnp.where((place >= 0) & (place < chunk), 1.0, 0.0).astype(BF16)

    def widen(values):
        return jnp.dot(values.astype(BF16), spread, preferred_element_type=F32)

    coarse = weight.astype(BF16).astype(F32)
    row = lax.rem(lax.broadcasted_iota(jnp.int32, (token_count, rows), 1), chunk)
    slot, backward = chunk_slot(row)
    hit = widen(rank) == slot
    ahead = jnp.where(backward, 0.0, jnp.where(hit, 1.0, 0.0))
    plan_ref[:token_count, :] = (widen(coarse) * ahead).astype(BF16)
    plan_ref[token_count : 2 * token_count, :] = (widen(weight - coarse) * ahead).astype(BF16)
    plan_ref[2 * token_count :, :] = jnp.where(backward & hit, 1.0, 0.0).astype(BF16)


def plan_unpack(routes, weights, experts, chunk):
    token_count = routes.shape[1]
    rows = experts * chunk
    return pl.pallas_call(
        lambda *refs: plan_kernel(experts, chunk, *refs),
        out_shape=jax.ShapeDtypeStruct((3 * token_count, rows), BF16),
        compiler_params=pltpu.CompilerParams(vmem_limit_bytes=32 * 1024 * 1024),
        cost_estimate=pl.CostEstimate(
            flops=6 * token_count * rows * experts, bytes_accessed=6 * token_count * rows, transcendentals=0
        ),
        interpret=INTERPRET,
        name="plan",
    )(routes, weights)


def unpack_kernel(plan_ref, back_ref, share_ref, mixed_ref, grad_ref, gate_ref, up_ref, down_ref):
    token_count = mixed_ref.shape[0]
    total = jnp.dot(plan_ref[...], back_ref[...], preferred_element_type=F32)
    mixed_ref[...] = (total[:token_count] + total[token_count : 2 * token_count]).astype(BF16)
    grad_ref[...] = total[2 * token_count :].astype(BF16)
    gate_ref[0] = share_ref[0].astype(F32)
    up_ref[0] = share_ref[1].astype(F32)
    down_ref[0] = share_ref[2].astype(F32).T


def unpack(plan, back, share):
    token_count = plan.shape[0] // 3
    rows, width = back.shape
    depth = share.shape[0]
    ffn = share.shape[1] // 3
    steps = 4
    block, part = width // steps, ffn // steps
    out = pl.BlockSpec((token_count, block), lambda j: (0, j))
    grad = pl.BlockSpec((1, depth, part), lambda j: (0, 0, j))
    return pl.pallas_call(
        lambda plan_ref, back_ref, gate_in, up_in, down_in, *refs: unpack_kernel(
            plan_ref, back_ref, (gate_in[...], up_in[...], down_in[...]), *refs
        ),
        grid=(steps,),
        in_specs=[
            pl.BlockSpec(plan.shape, lambda j: (0, 0)),
            pl.BlockSpec((rows, block), lambda j: (0, j)),
            pl.BlockSpec((depth, part), lambda j: (0, j)),
            pl.BlockSpec((depth, part), lambda j: (0, steps + j)),
            pl.BlockSpec((depth, part), lambda j: (0, 2 * steps + j)),
        ],
        out_specs=[out, out, grad, grad, pl.BlockSpec((1, part, depth), lambda j: (0, j, 0))],
        out_shape=[
            jax.ShapeDtypeStruct((token_count, width), BF16),
            jax.ShapeDtypeStruct((token_count, width), BF16),
            jax.ShapeDtypeStruct((1, depth, ffn), F32),
            jax.ShapeDtypeStruct((1, depth, ffn), F32),
            jax.ShapeDtypeStruct((1, ffn, depth), F32),
        ],
        compiler_params=pltpu.CompilerParams(vmem_limit_bytes=32 * 1024 * 1024),
        cost_estimate=pl.CostEstimate(
            flops=6 * token_count * rows * width, bytes_accessed=2 * (rows + 5 * token_count) * width, transcendentals=0
        ),
        interpret=INTERPRET,
        name="unpack",
    )(plan, back, share, share, share)


def weight_kernel(inputs_ref, grads_ref, pair_ref, hidden_ref, part_ref):
    contract_rows = (((0,), (0,)), ((), ()))
    both = pair_ref.shape[1]
    pair = lax.dot_general(inputs_ref[...], pair_ref[...], contract_rows, preferred_element_type=F32)
    part_ref[:, :both] = pair.astype(BF16)
    down = lax.dot_general(grads_ref[...], hidden_ref[...], contract_rows, preferred_element_type=F32)
    part_ref[:, both:] = down.astype(BF16)


def weight_parts(inputs, grads, pair_grads, hidden):
    slots, width = inputs.shape
    columns = pair_grads.shape[1] + hidden.shape[1]
    block = 256
    narrow = pl.BlockSpec((slots, block), lambda i: (0, i))
    whole = lambda array: pl.BlockSpec(array.shape, lambda i: (0, 0))
    return pl.pallas_call(
        weight_kernel,
        grid=(width // block,),
        in_specs=[narrow, narrow, whole(pair_grads), whole(hidden)],
        out_specs=pl.BlockSpec((block, columns), lambda i: (i, 0)),
        out_shape=jax.ShapeDtypeStruct((width, columns), BF16),
        compiler_params=pltpu.CompilerParams(vmem_limit_bytes=32 * 1024 * 1024),
        cost_estimate=pl.CostEstimate(
            flops=2 * slots * width * columns, bytes_accessed=2 * (slots + width) * columns, transcendentals=0
        ),
        interpret=INTERPRET,
        name="weight_parts",
    )(inputs, grads, pair_grads, hidden)


def roll_half(values):
    return pltpu.roll(values, 4, 1)


def expert_kernel(sources, inbox_ref, gate_ref, up_ref, down_ref, back_ref, tokens_ref, grads_ref, pair_ref, hidden_ref):
    width = inbox_ref.shape[1]
    ffn = gate_ref.shape[1]
    head = 8 * sources
    piece = 256
    for at in range(0, width, piece):
        cols = slice(at, at + piece)
        got = inbox_ref[:, cols].astype(F32).reshape(sources, 24, piece)
        both = got[:, 8:16].reshape(sources // 2, 2, 8, piece)
        first, second = both[:, 0], both[:, 1]
        low = lax.broadcasted_iota(jnp.int32, first.shape, 1) < 4
        tokens_ref[:head, cols] = got[:, :8].reshape(head, piece).astype(BF16)
        grads_ref[:head, cols] = got[:, 16:].reshape(head, piece).astype(BF16)
        tokens_ref[head:, cols] = jnp.where(low, first, roll_half(second)).reshape(-1, piece).astype(BF16)
        grads_ref[head:, cols] = jnp.where(low, roll_half(first), second).reshape(-1, piece).astype(BF16)
    tokens, grads = tokens_ref[...], grads_ref[...]
    gate_pre = jnp.dot(tokens, gate_ref[...], preferred_element_type=F32)
    up_pre = jnp.dot(tokens, up_ref[...], preferred_element_type=F32)
    hidden_grad = lax.dot_general(grads, down_ref[...], NT, preferred_element_type=F32)
    sigmoid = jax.nn.sigmoid(gate_pre)
    silu = gate_pre * sigmoid
    hidden = (silu * up_pre).astype(BF16)
    up_grad_pre = (hidden_grad * silu).astype(BF16)
    gate_grad_pre = (hidden_grad * up_pre * sigmoid * (1.0 + gate_pre * (1.0 - sigmoid))).astype(BF16)
    hidden_ref[...] = hidden
    pair_ref[:, :ffn] = gate_grad_pre
    pair_ref[:, ffn:] = up_grad_pre
    for at in range(0, width, piece):
        cols = slice(at, at + piece)
        outputs = jnp.dot(hidden, down_ref[:, cols], preferred_element_type=F32)
        slot = lax.dot_general(gate_grad_pre, gate_ref[cols, :], NT, preferred_element_type=F32)
        slot = slot + lax.dot_general(up_grad_pre, up_ref[cols, :], NT, preferred_element_type=F32)
        out_tail = outputs[head:].reshape(sources // 2, 8, piece)
        slot_tail = slot[head:].reshape(sources // 2, 8, piece)
        low = lax.broadcasted_iota(jnp.int32, out_tail.shape, 1) < 4
        first = jnp.where(low, out_tail, roll_half(slot_tail))
        second = jnp.where(low, roll_half(out_tail), slot_tail)
        middle = jnp.concatenate([first[:, None], second[:, None]], axis=1).reshape(sources, 8, piece)
        sent = jnp.concatenate(
            [outputs[:head].reshape(sources, 8, piece), middle, slot[:head].reshape(sources, 8, piece)], axis=1
        )
        back_ref[:, cols] = sent.reshape(24 * sources, piece).astype(BF16)


def run_expert(inbox, gate, up, down, sources, step):
    rows, width = inbox.shape
    ffn = gate.shape[1]
    slots = rows // 2
    part = lambda count, columns: pl.BlockSpec((count, columns), lambda i: (i, 0))
    whole = lambda array: pl.BlockSpec(array.shape, lambda i: (0, 0))
    many, few = 24 * step, 12 * step
    return pl.pallas_call(
        lambda *refs: expert_kernel(step, *refs),
        grid=(sources // step,),
        in_specs=[part(many, width), whole(gate), whole(up), whole(down)],
        out_specs=[part(many, width), part(few, width), part(few, width), part(few, 2 * ffn), part(few, ffn)],
        out_shape=[
            jax.ShapeDtypeStruct((rows, width), BF16),
            jax.ShapeDtypeStruct((slots, width), BF16),
            jax.ShapeDtypeStruct((slots, width), BF16),
            jax.ShapeDtypeStruct((slots, 2 * ffn), BF16),
            jax.ShapeDtypeStruct((slots, ffn), BF16),
        ],
        compiler_params=pltpu.CompilerParams(vmem_limit_bytes=48 * 1024 * 1024),
        cost_estimate=pl.CostEstimate(
            flops=12 * slots * width * ffn, bytes_accessed=14 * slots * width, transcendentals=slots * ffn
        ),
        interpret=INTERPRET,
        name="expert",
    )(inbox, gate, up, down)


def shards(tokens, routes, route_weights, gate_weight, up_weight, down_weight, cotangent):
    token_count, width = tokens.shape
    top_count = routes.shape[1]
    experts = lax.axis_size("expert")
    chunk = 2 * (token_count * top_count // experts)
    gate, up, down = gate_weight[0], up_weight[0], down_weight[0]

    def exchange(rows):
        moved = lax.all_to_all(rows.reshape(experts, chunk, width), "expert", split_axis=0, concat_axis=0, tiled=True)
        return moved.reshape(experts * chunk, width)

    choices, weights = routes.T, route_weights.T
    send = pack(tokens, cotangent, choices, weights, experts, chunk)
    inbox = exchange(send)
    back, inputs, out_grads, pair_grads, hidden = run_expert(inbox, gate, up, down, experts, 32)
    plan = plan_unpack(choices, weights, experts, chunk)
    returned = exchange(back)
    parts = weight_parts(inputs, out_grads, pair_grads, hidden)
    share = lax.psum_scatter(parts, "dp", scatter_dimension=0, tiled=True)
    return tuple(unpack(plan, returned, share))


def solution(mesh):
    rows = P(("dp", "expert"), None)
    expert = P("expert", None, None)
    return jax.shard_map(
        shards,
        mesh=mesh,
        in_specs=(rows, rows, rows, expert, expert, expert, rows),
        out_specs=(rows, rows, P("expert", "dp", None), P("expert", "dp", None), P("expert", None, "dp")),
        check_vma=False,
    )
```

time: 308 us -> 225 us (0.73)
  the two profiles are of different devices: /device:TPU:2 before, /device:TPU:114 now
where the time goes in v1:
time: 225 us
  blocking collectives  88.9 us (40%)
  waiting for transfers between devices  80.9 us (36%)
  Pallas kernels  19.1 us (8%)
  between operations  14.1 us (6%)
  starting transfers between devices  12 us (5%)
  local copies, waits for them, and re-layouts  9.39 us (4%)
    all_to_all x1, blocking collectives, exchange(): lax.all_to_all(rows.reshape(experts, chunk, width), 'expert', split_axis=...  88.9 us
    all_to_all x1, waiting for transfers between devices, exchange(): lax.all_to_all(rows.reshape(experts, chunk, width), 'expert', split_axis=...  80.9 us
    all_to_all x1, starting transfers between devices, exchange(): lax.all_to_all(rows.reshape(experts, chunk, width), 'expert', split_axis=...  12 us
    unnamed x28, local copies, waits for them, and re-layouts  9.39 us
    pallas_call x1, Pallas kernels, run_expert(): pl.pallas_call(lambda *refs: expert_kernel(step, *refs), grid=(sources //...  8.26 us
    pallas_call x1, Pallas kernels, weight_parts(): pl.pallas_call(weight_kernel, grid=(width // block,), in_specs=[narrow, n...  4.57 us
  transfers between devices with their start and end apart: 2, of which 1 were waited for; matrix products, arithmetic and copies ran while one was open for 0% of the time, Pallas kernels for 0%

profile of v1, /device:TPU:114, one launch (start us, length us, event | category | flops | bytes accessed | tf_op | source)
XLA Modules:
  0.0 224.5 jit_solution(2564897673593462684)
XLA Ops:
  7.2 0.0 reduce-scatter.2.cloned.1.call-start
  7.2 0.0 copy-start.3
  7.2 0.9 copy-done.3
  8.2 0.0 copy-start.4
  8.2 0.9 copy-done.4
  9.1 0.7 copy-done.5
  9.8 0.7 copy-done.7
  10.5 2.4 %pack.1 = bf16[1536,1024]{1,0:T(8,128)(2,1)S(1)} custom-call(s32[6,128]{1,0:T(8,128)S(1)} %bitcast.11, f32[6,128]{1,0:T(8,128)S(1)} %bitcast.13, bf16[128,1024]{1,0:T(8,128)(2,1)S(1)} %copy-done.3, bf16[128,1024]{1,0:T(8,128)(2,1)S(1)} %copy-done.4), custom_call_target="tpu_custom_call" | custom-call | flops 805306368 | bytes 3670016 | tf_op jit(solution)/shard_map/pack/pallas_call | solution.py:70
  12.9 0.0 copy-start.9
  12.9 0.0 copy-start.10
  12.9 0.0 copy-start.11
  12.9 88.9 %all_to_all.10 = bf16[64,24,1024]{2,1,0:T(8,128)(2,1)} all-to-all(bf16[64,24,1024]{2,1,0:T(8,128)(2,1)S(1)} %bitcast.9), channel_id=1, replica_groups=mesh['dp'=8,'expert'=64] {'expert'}, dimensions={0} | all-to-all | bytes 6291456 | tf_op jit(solution)/shard_map/all_to_all | solution.py:285
  101.8 0.0 copy-done.9
  101.8 0.0 copy-done.10
  101.8 0.0 copy-done.11
  101.8 8.3 %expert.1 = (bf16[1536,1024]{1,0:T(8,128)(2,1)}, bf16[768,1024]{1,0:T(8,128)(2,1)S(1)}, bf16[768,1024]{1,0:T(8,128)(2,1)}, bf16[768,1024]{1,0:T(8,128)(2,1)}, bf16[768,512]{1,0:T(8,128)(2,1)S(1)}) custom-call(bf16[1536,1024]{1,0:T(8,128)(2,1)} %bitcast.19, bf16[1024,512]{1,0:T(8,128)(2,1)S(1)} %bitcast.15, bf16[1024,512]{1,0:T(8,128)(2,1)S(1)} %bitcast.16, ...), custom_call_target="tpu_custom_call" | custom-call | flops 4831838208 | bytes 11010048 | tf_op jit(solution)/shard_map/expert/pallas_call | solution.py:256
  110.1 1.4 copy-done.12
  111.5 1.4 copy-done.13
  112.9 4.6 %weight_parts.1 = bf16[1024,1536]{1,0:T(8,128)(2,1)} custom-call(bf16[768,1024]{1,0:T(8,128)(2,1)S(1)} %get-tuple-element.11.inputs_ref, bf16[768,1024]{1,0:T(8,128)(2,1)S(1)} %copy-done.12, bf16[768,1024]{1,0:T(8,128)(2,1)S(1)} %copy-done.13, bf16[768,512]{1,0:T(8,128)(2,1)S(1)} %get-tuple-element.14.hidden_ref), custom_call_target="tpu_custom_call" | custom-call | flops 2415919104 | bytes 5505024 | tf_op jit(solution)/shard_map/weight_parts/pallas_call | solution.py:186
  117.4 0.0 reduce-scatter.2.cloned.1.call-update
  117.5 0.0 copy-start.6
  117.5 0.0 copy-start.8
  117.5 12.0 %all-to-all-start.1 = ((bf16[64,24,1024]{2,1,0:T(8,128)(2,1)}), bf16[64,24,1024]{2,1,0:T(8,128)(2,1)S(1)}, u32[]{:S(2)}, u32[]{:S(2)}) async-start(bf16[64,24,1024]{2,1,0:T(8,128)(2,1)} %bitcast.18), calls=%async_computation.1 | async-start | bytes 6291456 | tf_op jit(solution)/shard_map/all_to_all | solution.py:285
  129.5 0.0 copy-done.6
  129.5 0.0 copy-done.8
  129.5 0.7 plan.1.plan_ref
  130.2 0.0 copy-start
  130.3 1.0 copy-done
  131.3 80.9 %all-to-all-done.1 = bf16[64,24,1024]{2,1,0:T(8,128)(2,1)S(1)} async-done(((bf16[64,24,1024]{2,1,0:T(8,128)(2,1)}), bf16[64,24,1024]{2,1,0:T(8,128)(2,1)S(1)}, u32[]{:S(2)}, u32[]{:S(2)}) %all-to-all-start.1) | async-done | bytes 3145760 | tf_op jit(solution)/shard_map/all_to_all | solution.py:285
  212.2 1.3 copy-done.1
  213.5 1.0 copy-done.2
  214.5 3.2 %unpack.1 = (bf16[128,1024]{1,0:T(8,128)(2,1)}, bf16[128,1024]{1,0:T(8,128)(2,1)}, f32[1,128,512]{2,1,0:T(8,128)}, f32[1,128,512]{2,1,0:T(8,128)}, f32[1,512,128]{2,1,0:T(8,128)}) custom-call(bf16[384,1536]{1,0:T(8,128)(2,1)S(1)} %copy-done.1, bf16[1536,1024]{1,0:T(8,128)(2,1)S(1)} %bitcast.10, bf16[128,1536]{1,0:T(8,128)(2,1)S(1)} %copy-done.2, ...), custom_call_target="tpu_custom_call" | custom-call | flops 1207959552 | bytes 4456448 | tf_op jit(solution)/shard_map/unpack/pallas_call | solution.py:142
  (7 shorter events, 0.0 us)
Async XLA Ops:
  7.2 205.0 %reduce-scatter.2.cloned.1.call-start = ((), (), s32[]{:S(2)}) async-start(), calls=%async_computation.3 | async-start | bytes 3538944 | tf_op jit(solution)/shard_map/reduce_scatter | solution.py:295
  7.2 1.0 copy-start.3
  8.2 0.9 copy-start.4
  9.1 0.7 copy-start.5
  9.8 0.7 copy-start.7
  12.9 88.9 %copy-start.9 = (bf16[1,1024,512]{2,1,0:T(8,128)(2,1)S(1)}, bf16[1,1024,512]{2,1,0:T(8,128)(2,1)}, u32[]{:S(2)}) copy-start(bf16[1,1024,512]{2,1,0:T(8,128)(2,1)} %param.10) | copy-start | bytes 3145732
  12.9 88.9 %copy-start.10 = (bf16[1,1024,512]{2,1,0:T(8,128)(2,1)S(1)}, bf16[1,1024,512]{2,1,0:T(8,128)(2,1)}, u32[]{:S(2)}) copy-start(bf16[1,1024,512]{2,1,0:T(8,128)(2,1)} %param.11) | copy-start | bytes 3145732
  12.9 88.9 %copy-start.11 = (bf16[1,512,1024]{2,1,0:T(8,128)(2,1)S(1)}, bf16[1,512,1024]{2,1,0:T(8,128)(2,1)}, u32[]{:S(2)}) copy-start(bf16[1,512,1024]{2,1,0:T(8,128)(2,1)} %param.12) | copy-start | bytes 3145732
  110.1 1.4 copy-start.12
  111.5 1.4 copy-start.13
  117.5 12.0 %copy-start.6 = (s32[128,6]{0,1:T(8,128)S(1)}, s32[128,6]{0,1:T(8,128)}, u32[]{:S(2)}) copy-start(s32[128,6]{0,1:T(8,128)} %param.8) | copy-start | bytes 9220
  117.5 12.0 %copy-start.8 = (f32[128,6]{0,1:T(8,128)S(1)}, f32[128,6]{0,1:T(8,128)}, u32[]{:S(2)}) copy-start(f32[128,6]{0,1:T(8,128)} %param.9) | copy-start | bytes 9220
  117.5 94.7 %all-to-all-start.1 = ((bf16[64,24,1024]{2,1,0:T(8,128)(2,1)}), bf16[64,24,1024]{2,1,0:T(8,128)(2,1)S(1)}, u32[]{:S(2)}, u32[]{:S(2)}) async-start(bf16[64,24,1024]{2,1,0:T(8,128)(2,1)} %bitcast.18), calls=%async_computation.1 | async-start | bytes 6291456 | tf_op jit(solution)/shard_map/all_to_all | solution.py:285
  130.2 1.0 copy-start
  212.2 1.3 copy-start.1
  213.5 1.0 copy-start.2
Sparse Core Ops, SparseCore 0:
  117.6 38.3 reduce-scatter.1

commit v2 on v1

v2 whole, which is shorter than its diff:
```python
import jax
import jax.numpy as jnp
from jax import lax
from jax.experimental import pallas as pl
from jax.experimental.pallas import tpu as pltpu
from jax.sharding import PartitionSpec as P

INTERPRET = False
PACK_STEPS = 2
EXPERT_STEP = 32
F32 = jnp.float32
BF16 = jnp.bfloat16
NT = (((1,), (1,)), ((), ()))
HBM = pltpu.MemorySpace.HBM
VMEM = pltpu.MemorySpace.VMEM


def placed(array, space):
    return array if INTERPRET else pltpu.with_memory_space_constraint(array, space)


def made(shape, dtype, space):
    return jax.ShapeDtypeStruct(shape, dtype) if INTERPRET else space(shape, dtype)


def chunk_slot(row):
    slot = jnp.where(row < 12, row, jnp.where(row < 16, row - 4, row - 16))
    return slot.astype(F32), row >= 12


SIDE = 8


def expert_at(place):
    across, along = place // SIDE, place % SIDE
    return along * SIDE + (across + along) % SIDE


def route_tables(routes, weights, experts):
    top_count, token_count = routes.shape
    expert = expert_at(lax.broadcasted_iota(jnp.int32, (experts, token_count), 0))
    named = jnp.zeros((experts, token_count), F32)
    weight = jnp.zeros((experts, token_count), F32)
    for k in range(top_count):
        same = routes[k : k + 1, :] == expert
        named = jnp.where(same, 1.0, named)
        weight = jnp.where(same, weights[k : k + 1, :], weight)
    earlier = lax.broadcasted_iota(jnp.int32, (token_count, token_count), 0)
    later = lax.broadcasted_iota(jnp.int32, (token_count, token_count), 1)
    before = jnp.where(earlier < later, 1.0, 0.0).astype(BF16)
    rank = jnp.dot(named.astype(BF16), before, preferred_element_type=F32)
    return jnp.where(named > 0.0, rank, -1.0), weight


def pack_kernel(
    chunk, routes_hbm, weights_hbm, tokens_hbm, cot_hbm, send_ref, routes, weights, rows, rank_ref, weight_ref, sems
):
    token_count = routes.shape[1]
    total = rank_ref.shape[0]
    experts = send_ref.shape[0] // chunk
    step = pl.program_id(0)

    @pl.when(step == 0)
    def _():
        moves = [
            pltpu.make_async_copy(source, target, sems.at[i])
            for i, (source, target) in enumerate(
                [
                    (routes_hbm, routes),
                    (weights_hbm, weights),
                    (tokens_hbm, rows.at[pl.ds(0, token_count)]),
                    (cot_hbm, rows.at[pl.ds(token_count, token_count)]),
                ]
            )
        ]
        for move in moves:
            move.start()
        moves[0].wait()
        moves[1].wait()
        rank_ref[...], weight_ref[...] = route_tables(routes[...], weights[...], total)
        moves[2].wait()
        moves[3].wait()

    here = pl.ds(pl.multiple_of(step * experts, experts), experts)
    full = (experts, chunk, token_count)
    slot, backward = chunk_slot(lax.broadcasted_iota(jnp.int32, full, 1))
    hit = jnp.broadcast_to(rank_ref[here][:, None, :], full) == slot
    one = jnp.where(hit, 1.0, 0.0)
    forward_pick = jnp.where(backward, 0.0, one).reshape(experts * chunk, token_count).astype(BF16)
    backward_pick = jnp.where(backward, one, 0.0).reshape(experts * chunk, token_count).astype(BF16)
    chosen = jnp.where(hit, jnp.broadcast_to(weight_ref[here][:, None, :], full), 0.0)
    scale = jnp.where(backward, jnp.sum(chosen, axis=2, keepdims=True), 1.0).reshape(experts * chunk, token_count)
    pick = jnp.concatenate([forward_pick, backward_pick], axis=1)
    picked = jnp.dot(pick, rows[...], preferred_element_type=F32)
    for at in range(0, picked.shape[1], token_count):
        send_ref[:, at : at + token_count] = (picked[:, at : at + token_count] * scale).astype(BF16)


def pack(tokens, cotangent, routes, weights, experts, chunk):
    token_count, width = tokens.shape
    rows = experts * chunk
    steps = PACK_STEPS
    hbm = pl.BlockSpec(memory_space=pltpu.MemorySpace.HBM)
    return pl.pallas_call(
        lambda *refs: pack_kernel(chunk, *refs),
        grid=(steps,),
        in_specs=[hbm, hbm, hbm, hbm],
        out_specs=pl.BlockSpec((rows // steps, width), lambda i: (i, 0)),
        out_shape=jax.ShapeDtypeStruct((rows, width), BF16),
        scratch_shapes=[
            pltpu.VMEM(routes.shape, jnp.int32),
            pltpu.VMEM(weights.shape, F32),
            pltpu.VMEM((2 * token_count, width), BF16),
            pltpu.VMEM((experts, token_count), F32),
            pltpu.VMEM((experts, token_count), F32),
            pltpu.SemaphoreType.DMA((4,)),
        ],
        compiler_params=pltpu.CompilerParams(vmem_limit_bytes=28 * 1024 * 1024),
        cost_estimate=pl.CostEstimate(
            flops=4 * rows * token_count * width, bytes_accessed=2 * (rows + 2 * token_count) * width, transcendentals=0
        ),
        interpret=INTERPRET,
        name="pack",
    )(*(placed(array, HBM) for array in (routes, weights, tokens, cotangent)))


def plan_kernel(experts, chunk, routes_ref, weights_ref, plan_ref):
    token_count = routes_ref.shape[1]
    rank, weight = route_tables(routes_ref[...], weights_ref[...], 128)
    rank, weight = rank.T[:, :experts], weight.T[:, :experts]
    rows = experts * chunk
    owner = lax.broadcasted_iota(jnp.int32, (experts, rows), 0) * chunk
    place = lax.broadcasted_iota(jnp.int32, (experts, rows), 1) - owner
    spread = jnp.where((place >= 0) & (place < chunk), 1.0, 0.0).astype(BF16)

    def widen(values):
        return jnp.dot(values.astype(BF16), spread, preferred_element_type=F32)

    coarse = weight.astype(BF16).astype(F32)
    row = lax.rem(lax.broadcasted_iota(jnp.int32, (token_count, rows), 1), chunk)
    slot, backward = chunk_slot(row)
    hit = widen(rank) == slot
    ahead = jnp.where(backward, 0.0, jnp.where(hit, 1.0, 0.0))
    plan_ref[:token_count, :] = (widen(coarse) * ahead).astype(BF16)
    plan_ref[token_count : 2 * token_count, :] = (widen(weight - coarse) * ahead).astype(BF16)
    plan_ref[2 * token_count :, :] = jnp.where(backward & hit, 1.0, 0.0).astype(BF16)


def plan_unpack(routes, weights, experts, chunk):
    token_count = routes.shape[1]
    rows = experts * chunk
    return pl.pallas_call(
        lambda *refs: plan_kernel(experts, chunk, *refs),
        out_shape=jax.ShapeDtypeStruct((3 * token_count, rows), BF16),
        compiler_params=pltpu.CompilerParams(vmem_limit_bytes=28 * 1024 * 1024),
        cost_estimate=pl.CostEstimate(
            flops=6 * token_count * rows * experts, bytes_accessed=6 * token_count * rows, transcendentals=0
        ),
        interpret=INTERPRET,
        name="plan",
    )(routes, weights)


def unpack_kernel(plan_ref, back_ref, mixed_ref, grad_ref):
    token_count, width = mixed_ref.shape
    piece = 256
    for at in range(0, width, piece):
        cols = slice(at, at + piece)
        total = jnp.dot(plan_ref[...], back_ref[:, cols], preferred_element_type=F32)
        mixed_ref[:, cols] = (total[:token_count] + total[token_count : 2 * token_count]).astype(BF16)
        grad_ref[:, cols] = total[2 * token_count :].astype(BF16)


def unpack(plan, back):
    token_count = plan.shape[0] // 3
    rows, width = back.shape
    here = pl.BlockSpec(memory_space=VMEM)
    return pl.pallas_call(
        unpack_kernel,
        in_specs=[here, here],
        out_specs=[here, here],
        out_shape=[jax.ShapeDtypeStruct((token_count, width), BF16)] * 2,
        compiler_params=pltpu.CompilerParams(vmem_limit_bytes=28 * 1024 * 1024),
        cost_estimate=pl.CostEstimate(
            flops=6 * token_count * rows * width, bytes_accessed=2 * (rows + 5 * token_count) * width, transcendentals=0
        ),
        interpret=INTERPRET,
        name="unpack",
    )(placed(plan, VMEM), placed(back, VMEM))


def shard_dots(inputs_ref, grads_ref, pair_ref, hidden_ref):
    contract_rows = (((0,), (0,)), ((), ()))
    pair = lax.dot_general(inputs_ref[...], pair_ref[...], contract_rows, preferred_element_type=F32)
    down = lax.dot_general(grads_ref[...], hidden_ref[...], contract_rows, preferred_element_type=F32)
    return pair, down


def weight_kernel(first, place_ref, inputs_ref, grads_ref, pair_ref, hidden_ref, *refs):
    part_ref = refs[-1]
    both = pair_ref.shape[1]
    pair, down = shard_dots(inputs_ref, grads_ref, pair_ref, hidden_ref)
    if not first:
        pair = pair + refs[0][0, :, :both].astype(F32)
        down = down + refs[0][0, :, both:].astype(F32)
    part_ref[0, :, :both] = pair.astype(BF16)
    part_ref[0, :, both:] = down.astype(BF16)


def weight_half(place, inputs, grads, pair_grads, hidden, arrived, chips):
    slots, width = inputs.shape
    columns = pair_grads.shape[1] + hidden.shape[1]
    depth = width // (2 * chips)
    narrow = pl.BlockSpec((slots, depth), lambda i, at: (0, lax.rem(at[0] + i, chips) * 2 + at[1]))
    whole = lambda array: pl.BlockSpec(array.shape, lambda i, at: (0, 0))
    part = pl.BlockSpec((1, depth, columns), lambda i, at: (i, 0, 0))
    extra = [] if arrived is None else [arrived]
    return pl.pallas_call(
        lambda *refs: weight_kernel(arrived is None, *refs),
        grid_spec=pltpu.PrefetchScalarGridSpec(
            num_scalar_prefetch=1,
            grid=(chips,),
            in_specs=[narrow, narrow, whole(pair_grads), whole(hidden)] + [part for _ in extra],
            out_specs=part,
        ),
        out_shape=jax.ShapeDtypeStruct((chips, depth, columns), BF16),
        compiler_params=pltpu.CompilerParams(vmem_limit_bytes=28 * 1024 * 1024),
        cost_estimate=pl.CostEstimate(
            flops=slots * width * columns, bytes_accessed=2 * (slots + width) * columns, transcendentals=0
        ),
        interpret=INTERPRET,
        name="weight_half",
    )(place, inputs, grads, pair_grads, hidden, *extra)


def finish_kernel(*refs):
    gate_ref, up_ref, down_ref = refs[-3:]
    total = refs[0][0].astype(F32)
    for ref in refs[1:-3]:
        total = total + ref[0].astype(F32)
    ffn = gate_ref.shape[2]
    gate_ref[0] = total[:, :ffn]
    up_ref[0] = total[:, ffn : 2 * ffn]
    down_ref[0] = total[:, 2 * ffn :].T


def finish(shards_of):
    _, depth, columns = shards_of[0].shape
    ffn = columns // 3
    one = pl.BlockSpec((1, depth, columns), lambda: (0, 0, 0))
    return pl.pallas_call(
        finish_kernel,
        in_specs=[one for _ in shards_of],
        out_shape=[
            jax.ShapeDtypeStruct((1, depth, ffn), F32),
            jax.ShapeDtypeStruct((1, depth, ffn), F32),
            jax.ShapeDtypeStruct((1, ffn, depth), F32),
        ],
        compiler_params=pltpu.CompilerParams(vmem_limit_bytes=28 * 1024 * 1024),
        cost_estimate=pl.CostEstimate(
            flops=4 * depth * columns, bytes_accessed=12 * depth * columns, transcendentals=0
        ),
        interpret=INTERPRET,
        name="finish",
    )(*shards_of)


def roll_half(values):
    return pltpu.roll(values, 4, 1)


def split_slots(inbox_ref, tokens_ref, grads_ref):
    rows, width = inbox_ref.shape
    sources = rows // 24
    head = 8 * sources
    piece = 256
    for at in range(0, width, piece):
        cols = slice(at, at + piece)
        got = inbox_ref[:, cols].astype(F32).reshape(sources, 24, piece)
        both = got[:, 8:16].reshape(sources // 2, 2, 8, piece)
        first, second = both[:, 0], both[:, 1]
        low = lax.broadcasted_iota(jnp.int32, first.shape, 1) < 4
        tokens_ref[:head, cols] = got[:, :8].reshape(head, piece).astype(BF16)
        grads_ref[:head, cols] = got[:, 16:].reshape(head, piece).astype(BF16)
        tokens_ref[head:, cols] = jnp.where(low, first, roll_half(second)).reshape(-1, piece).astype(BF16)
        grads_ref[head:, cols] = jnp.where(low, roll_half(first), second).reshape(-1, piece).astype(BF16)


def sort_slots(inbox, sources, step):
    rows, width = inbox.shape
    slots = rows // 2
    part = lambda count: pl.BlockSpec((count, width), lambda i: (i, 0))
    return pl.pallas_call(
        split_slots,
        grid=(sources // step,),
        in_specs=[part(24 * step)],
        out_specs=[part(12 * step), part(12 * step)],
        out_shape=[jax.ShapeDtypeStruct((slots, width), BF16)] * 2,
        compiler_params=pltpu.CompilerParams(vmem_limit_bytes=28 * 1024 * 1024),
        cost_estimate=pl.CostEstimate(flops=4 * rows * width, bytes_accessed=4 * rows * width, transcendentals=0),
        interpret=INTERPRET,
        name="sort_slots",
    )(inbox)


def expert_kernel(
    sources, inbox_all, gate_ref, up_ref, down_ref, back_ref, pair_ref, hidden_ref, tokens_ref, grads_ref
):
    many = 24 * sources
    inbox_ref = inbox_all.at[pl.ds(pl.multiple_of(pl.program_id(0) * many, many), many)]
    width = inbox_ref.shape[1]
    ffn = gate_ref.shape[1]
    head = 8 * sources
    piece = 256
    split_slots(inbox_ref, tokens_ref, grads_ref)
    tokens, grads = tokens_ref[...], grads_ref[...]
    gate_pre = jnp.dot(tokens, gate_ref[...], preferred_element_type=F32)
    up_pre = jnp.dot(tokens, up_ref[...], preferred_element_type=F32)
    hidden_grad = lax.dot_general(grads, down_ref[...], NT, preferred_element_type=F32)
    sigmoid = jax.nn.sigmoid(gate_pre)
    silu = gate_pre * sigmoid
    hidden = (silu * up_pre).astype(BF16)
    up_grad_pre = (hidden_grad * silu).astype(BF16)
    gate_grad_pre = (hidden_grad * up_pre * sigmoid * (1.0 + gate_pre * (1.0 - sigmoid))).astype(BF16)
    hidden_ref[...] = hidden
    pair_ref[:, :ffn] = gate_grad_pre
    pair_ref[:, ffn:] = up_grad_pre
    for at in range(0, width, piece):
        cols = slice(at, at + piece)
        outputs = jnp.dot(hidden, down_ref[:, cols], preferred_element_type=F32)
        slot = lax.dot_general(gate_grad_pre, gate_ref[cols, :], NT, preferred_element_type=F32)
        slot = slot + lax.dot_general(up_grad_pre, up_ref[cols, :], NT, preferred_element_type=F32)
        out_tail = outputs[head:].reshape(sources // 2, 8, piece)
        slot_tail = slot[head:].reshape(sources // 2, 8, piece)
        low = lax.broadcasted_iota(jnp.int32, out_tail.shape, 1) < 4
        first = jnp.where(low, out_tail, roll_half(slot_tail))
        second = jnp.where(low, roll_half(out_tail), slot_tail)
        middle = jnp.concatenate([first[:, None], second[:, None]], axis=1).reshape(sources, 8, piece)
        sent = jnp.concatenate(
            [outputs[:head].reshape(sources, 8, piece), middle, slot[:head].reshape(sources, 8, piece)], axis=1
        )
        back_ref[:, cols] = sent.reshape(24 * sources, piece).astype(BF16)


def run_expert(inbox, gate, up, down, sources, step):
    rows, width = inbox.shape
    ffn = gate.shape[1]
    slots = rows // 2
    part = lambda count, columns: pl.BlockSpec((count, columns), lambda i: (i, 0))
    here = pl.BlockSpec(memory_space=VMEM)
    many, few = 24 * step, 12 * step
    return pl.pallas_call(
        lambda *refs: expert_kernel(step, *refs),
        grid=(sources // step,),
        in_specs=[here, here, here, here],
        out_specs=[part(many, width), part(few, 2 * ffn), part(few, ffn)],
        out_shape=[
            made((rows, width), BF16, HBM),
            made((slots, 2 * ffn), BF16, HBM),
            made((slots, ffn), BF16, HBM),
        ],
        scratch_shapes=[
            pltpu.VMEM((few, width), BF16),
            pltpu.VMEM((few, width), BF16),
        ],
        compiler_params=pltpu.CompilerParams(vmem_limit_bytes=28 * 1024 * 1024),
        cost_estimate=pl.CostEstimate(
            flops=12 * slots * width * ffn, bytes_accessed=14 * slots * width, transcendentals=slots * ffn
        ),
        interpret=INTERPRET,
        name="expert",
    )(*(placed(array, VMEM) for array in (inbox, gate, up, down)))


def shards(tokens, routes, route_weights, gate_weight, up_weight, down_weight, cotangent):
    token_count, width = tokens.shape
    top_count = routes.shape[1]
    experts = lax.axis_size("expert")
    chunk = 2 * (token_count * top_count // experts)
    gate, up, down = gate_weight[0], up_weight[0], down_weight[0]

    order = [[expert_at(place) for place in range(experts)]]

    def exchange(rows):
        moved = lax.all_to_all(rows.reshape(experts, chunk, width), "expert", split_axis=0, concat_axis=0, tiled=True, axis_index_groups=order)
        return moved.reshape(experts * chunk, width)

    choices, weights = routes.T, route_weights.T
    send = pack(tokens, cotangent, choices, weights, experts, chunk)
    inbox = exchange(send)
    back, pair_grads, hidden = run_expert(inbox, gate, up, down, experts, EXPERT_STEP)
    inputs, out_grads = sort_slots(inbox, experts, EXPERT_STEP)
    plan = plan_unpack(choices, weights, experts, chunk)
    returned = exchange(back)
    groups = lax.axis_size("dp")
    chips = groups // 2
    me = lax.axis_index("dp")
    chip, core = me // 2, me % 2
    work = (inputs, out_grads, pair_grads, hidden)
    other = weight_half(jnp.stack([chip, 1 - core]).astype(jnp.int32), *work, None, chips)
    arrived = lax.ppermute(other, "dp", [(d, d ^ 1) for d in range(groups)])
    mine = weight_half(jnp.stack([chip, core]).astype(jnp.int32), *work, arrived, chips)
    pieces = [mine[:1]]
    for step in range(1, chips):
        hop = [(d, (d + 2 * step) % groups) for d in range(groups)]
        pieces.append(lax.ppermute(mine[step : step + 1], "dp", hop))
    mixed_latent, latent_grad = unpack(plan, returned)
    return (mixed_latent, latent_grad, *finish(pieces))


def solution(mesh):
    rows = P(("dp", "expert"), None)
    expert = P("expert", None, None)
    return jax.shard_map(
        shards,
        mesh=mesh,
        in_specs=(rows, rows, rows, expert, expert, expert, rows),
        out_specs=(rows, rows, P("expert", "dp", None), P("expert", "dp", None), P("expert", None, "dp")),
        check_vma=False,
    )
```

time: 225 us -> 199 us (0.88)
  the two profiles are of different devices: /device:TPU:114 before, /device:TPU:46 now
where the time goes in v2:
time: 199 us
  blocking collectives  90.9 us (46%)
  waiting for transfers between devices  63.9 us (32%)
  Pallas kernels  21.7 us (11%)
  starting transfers between devices  20 us (10%)
    all_to_all x1, blocking collectives, exchange(): lax.all_to_all(rows.reshape(experts, chunk, width), 'expert', split_axis=...  90.9 us
    all_to_all x1, waiting for transfers between devices, exchange(): lax.all_to_all(rows.reshape(experts, chunk, width), 'expert', split_axis=...  45 us
    ppermute x3, waiting for transfers between devices, shards(): pieces.append(lax.ppermute(mine[step:step + 1], 'dp', hop))  15.6 us
    all_to_all x1, starting transfers between devices, exchange(): lax.all_to_all(rows.reshape(experts, chunk, width), 'expert', split_axis=...  9.41 us
    ppermute x3, starting transfers between devices, shards(): pieces.append(lax.ppermute(mine[step:step + 1], 'dp', hop))  8.7 us
    pallas_call x1, Pallas kernels, run_expert(): pl.pallas_call(lambda *refs: expert_kernel(step, *refs), grid=(sources //...  6.82 us
    pallas_call x2, Pallas kernels, weight_half(): pl.pallas_call(lambda *refs: weight_kernel(arrived is None, *refs), grid_...  6.3 us
    pallas_call x1, Pallas kernels, unpack(): pl.pallas_call(unpack_kernel, in_specs=[here, here], out_specs=[here, her...  4.03 us
  transfers between devices with their start and end apart: 5, of which 5 were waited for; matrix products, arithmetic and copies ran while one was open for 0% of the time, Pallas kernels for 4%

profile of v2, /device:TPU:46, one launch (start us, length us, event | category | flops | bytes accessed | tf_op | source)
XLA Modules:
  0.0 198.7 jit_solution(12524670552709005970)
XLA Ops:
  0.6 2.3 %pack.1 = bf16[1536,1024]{1,0:T(8,128)(2,1)S(1)} custom-call(s32[6,128]{1,0:T(8,128)} %bitcast.15, f32[6,128]{1,0:T(8,128)} %bitcast.17, bf16[128,1024]{1,0:T(8,128)(2,1)} %refs_2_.1, bf16[128,1024]{1,0:T(8,128)(2,1)} %refs_3_.1), custom_call_target="tpu_custom_call" | custom-call | flops 805306368 | bytes 3670016 | tf_op jit(solution)/shard_map/pack/pallas_call | solution.py:104
  2.9 0.0 copy-start.4
  2.9 0.0 copy-start.5
  3.0 0.0 copy-start.6
  3.0 90.9 %all_to_all.10 = bf16[64,24,1024]{2,1,0:T(8,128)(2,1)S(1)} all-to-all(bf16[64,24,1024]{2,1,0:T(8,128)(2,1)S(1)} %bitcast.14), channel_id=1, replica_groups={{0,9,18,27,36,45,54,63,1,10,19,28,37,46,55,56,2,11,20,29,38,47,48,57,3,..., dimensions={0} | all-to-all | bytes 6291456 | tf_op jit(solution)/shard_map/all_to_all | solution.py:385
  93.9 0.0 copy-done.4
  93.9 0.0 copy-done.5
  93.9 0.0 copy-done.6
  93.9 6.8 %expert.1 = (bf16[1536,1024]{1,0:T(8,128)(2,1)}, bf16[768,1024]{1,0:T(8,128)(2,1)}, bf16[768,512]{1,0:T(8,128)(2,1)}) custom-call(bf16[1536,1024]{1,0:T(8,128)(2,1)S(1)} %bitcast.12, bf16[1024,512]{1,0:T(8,128)(2,1)S(1)} %bitcast.19, bf16[1024,512]{1,0:T(8,128)(2,1)S(1)} %bitcast.20, bf16[512,1024]{1,0:T(8,128)(2,1)S(1)} %bitcast.21), custom_call_target="tpu_custom_call" | custom-call | flops 4831838208 | bytes 11010048 | tf_op jit(solution)/shard_map/expert/pallas_call | solution.py:352
  100.7 9.4 %all-to-all-start.1 = ((bf16[64,24,1024]{2,1,0:T(8,128)(2,1)}), bf16[64,24,1024]{2,1,0:T(8,128)(2,1)}, u32[]{:S(2)}, u32[]{:S(2)}) async-start(bf16[64,24,1024]{2,1,0:T(8,128)(2,1)} %bitcast.22), calls=%async_computation.1 | async-start | bytes 6291456 | tf_op jit(solution)/shard_map/all_to_all | solution.py:385
  110.2 0.1 pad_add_fusion.1.refs_0_
  110.2 0.5 sort_slots.1
  110.7 0.9 copy-done
  111.6 0.2 copy-done.1
  111.8 3.1 %weight_half.2 = bf16[4,128,1536]{2,1,0:T(8,128)(2,1)S(1)} custom-call(s32[2]{0:T(128)S(1)} %pad_add_fusion.1.refs_0_, bf16[768,1024]{1,0:T(8,128)(2,1)S(1)} %get-tuple-element.18.refs_1_, bf16[768,1024]{1,0:T(8,128)(2,1)S(1)} %get-tuple-element.19.refs_2_, bf16[768,1024]{1,0:T(8,128)(2,1)S(1)} %copy-done, bf16[768,512]{1,0:T(8,128)(2,1)S(1)} %copy-done.1), custom_call_target="tpu_custom_call" | custom-call | flops 1207959552 | bytes 5505024 | tf_op jit(solution)/shard_map/weight_half/pallas_call | solution.py:218
  115.0 1.9 collective-permute-start
  116.9 0.1 pad_add_fusion.refs_0_
  117.0 3.3 %collective-permute-done.refs_5_ = bf16[4,128,1536]{2,1,0:T(8,128)(2,1)S(1)} collective-permute-done((bf16[4,128,1536]{2,1,0:T(8,128)(2,1)S(1)}, bf16[4,128,1536]{2,1,0:T(8,128)(2,1)S(1)}, u32[]{:S(2)}, u32[]{:S(2)}) %collective-permute-start) | collective-permute-done | bytes 1572896 | tf_op jit(solution)/shard_map/ppermute | solution.py:401
  120.3 3.1 %weight_half.3 = bf16[4,128,1536]{2,1,0:T(8,128)(2,1)S(1)} custom-call(s32[2]{0:T(128)S(1)} %pad_add_fusion.refs_0_, bf16[768,1024]{1,0:T(8,128)(2,1)S(1)} %get-tuple-element.18.refs_1_, bf16[768,1024]{1,0:T(8,128)(2,1)S(1)} %get-tuple-element.19.refs_2_, bf16[768,1024]{1,0:T(8,128)(2,1)S(1)} %copy-done, bf16[768,512]{1,0:T(8,128)(2,1)S(1)} %copy-done.1, ...), custom_call_target="tpu_custom_call" | custom-call | flops 1207959552 | bytes 5505024 | tf_op jit(solution)/shard_map/weight_half/pallas_call | solution.py:218
  123.5 0.0 copy-start.2
  123.5 0.0 copy-start.3
  123.5 0.1 fusion
  123.6 2.4 %collective-permute-start.1 = (bf16[1,128,1536]{2,1,0:T(8,128)(2,1)S(1)}, bf16[1,128,1536]{2,1,0:T(8,128)(2,1)S(1)}, u32[]{:S(2)}, u32[]{:S(2)}) collective-permute-start(bf16[1,128,1536]{2,1,0:T(8,128)(2,1)S(1)} %get-tuple-element.27), channel_id=1, source_target_pairs={{0,128},{64,192},{128,256},{192,320},{256,384},{320,448},{384,0},{... | collective-permute-start | bytes 1179656 | tf_op jit(solution)/shard_map/ppermute | solution.py:406
  126.0 4.4 %collective-permute-start.2 = (bf16[1,128,1536]{2,1,0:T(8,128)(2,1)S(1)}, bf16[1,128,1536]{2,1,0:T(8,128)(2,1)S(1)}, u32[]{:S(2)}, u32[]{:S(2)}) collective-permute-start(bf16[1,128,1536]{2,1,0:T(8,128)(2,1)S(1)} %get-tuple-element.26), channel_id=1, source_target_pairs={{0,256},{64,320},{128,384},{192,448},{256,0},{320,64},{384,128},{4... | collective-permute-start | bytes 1179656 | tf_op jit(solution)/shard_map/ppermute | solution.py:406
  130.4 1.9 collective-permute-start.3
  132.3 0.7 plan.1.plan_ref
  133.1 4.4 %collective-permute-done.1.refs_1_ = bf16[1,128,1536]{2,1,0:T(8,128)(2,1)S(1)} collective-permute-done((bf16[1,128,1536]{2,1,0:T(8,128)(2,1)S(1)}, bf16[1,128,1536]{2,1,0:T(8,128)(2,1)S(1)}, u32[]{:S(2)}, u32[]{:S(2)}) %collective-permute-start.1) | collective-permute-done | bytes 393248 | tf_op jit(solution)/shard_map/ppermute | solution.py:406
  137.5 4.0 %collective-permute-done.2.refs_2_ = bf16[1,128,1536]{2,1,0:T(8,128)(2,1)S(1)} collective-permute-done((bf16[1,128,1536]{2,1,0:T(8,128)(2,1)S(1)}, bf16[1,128,1536]{2,1,0:T(8,128)(2,1)S(1)}, u32[]{:S(2)}, u32[]{:S(2)}) %collective-permute-start.2) | collective-permute-done | bytes 393248 | tf_op jit(solution)/shard_map/ppermute | solution.py:406
  141.5 7.3 %collective-permute-done.3.refs_3_ = bf16[1,128,1536]{2,1,0:T(8,128)(2,1)S(1)} collective-permute-done((bf16[1,128,1536]{2,1,0:T(8,128)(2,1)S(1)}, bf16[1,128,1536]{2,1,0:T(8,128)(2,1)S(1)}, u32[]{:S(2)}, u32[]{:S(2)}) %collective-permute-start.3) | collective-permute-done | bytes 393248 | tf_op jit(solution)/shard_map/ppermute | solution.py:406
  148.7 1.0 finish.1
  149.7 45.0 %all-to-all-done.1 = bf16[64,24,1024]{2,1,0:T(8,128)(2,1)} async-done(((bf16[64,24,1024]{2,1,0:T(8,128)(2,1)}), bf16[64,24,1024]{2,1,0:T(8,128)(2,1)}, u32[]{:S(2)}, u32[]{:S(2)}) %all-to-all-start.1) | async-done | bytes 3145760 | tf_op jit(solution)/shard_map/all_to_all | solution.py:385
  194.7 4.0 %unpack.1 = (bf16[128,1024]{1,0:T(8,128)(2,1)}, bf16[128,1024]{1,0:T(8,128)(2,1)}) custom-call(bf16[384,1536]{1,0:T(8,128)(2,1)S(1)} %plan.1.plan_ref, bf16[1536,1024]{1,0:T(8,128)(2,1)} %bitcast.8.back_ref), custom_call_target="tpu_custom_call" | custom-call | flops 1207959552 | bytes 4456448 | tf_op jit(solution)/shard_map/unpack/pallas_call | solution.py:178
  (4 shorter events, 0.0 us)
Async XLA Ops:
  2.9 91.0 %copy-start.4 = (bf16[1,1024,512]{2,1,0:T(8,128)(2,1)S(1)}, bf16[1,1024,512]{2,1,0:T(8,128)(2,1)}, u32[]{:S(2)}) copy-start(bf16[1,1024,512]{2,1,0:T(8,128)(2,1)} %param.10) | copy-start | bytes 3145732
  2.9 91.0 %copy-start.5 = (bf16[1,1024,512]{2,1,0:T(8,128)(2,1)S(1)}, bf16[1,1024,512]{2,1,0:T(8,128)(2,1)}, u32[]{:S(2)}) copy-start(bf16[1,1024,512]{2,1,0:T(8,128)(2,1)} %param.11) | copy-start | bytes 3145732
  3.0 90.9 %copy-start.6 = (bf16[1,512,1024]{2,1,0:T(8,128)(2,1)S(1)}, bf16[1,512,1024]{2,1,0:T(8,128)(2,1)}, u32[]{:S(2)}) copy-start(bf16[1,512,1024]{2,1,0:T(8,128)(2,1)} %param.12) | copy-start | bytes 3145732
  100.7 94.0 %all-to-all-start.1 = ((bf16[64,24,1024]{2,1,0:T(8,128)(2,1)}), bf16[64,24,1024]{2,1,0:T(8,128)(2,1)}, u32[]{:S(2)}, u32[]{:S(2)}) async-start(bf16[64,24,1024]{2,1,0:T(8,128)(2,1)} %bitcast.22), calls=%async_computation.1 | async-start | bytes 6291456 | tf_op jit(solution)/shard_map/all_to_all | solution.py:385
  110.2 1.4 copy-start
  110.2 1.6 copy-start.1
  115.0 5.3 %collective-permute-start = (bf16[4,128,1536]{2,1,0:T(8,128)(2,1)S(1)}, bf16[4,128,1536]{2,1,0:T(8,128)(2,1)S(1)}, u32[]{:S(2)}, u32[]{:S(2)}) collective-permute-start(bf16[4,128,1536]{2,1,0:T(8,128)(2,1)S(1)} %weight_half.2), channel_id=1, source_target_pairs={{0,64},{64,0},{128,192},{192,128},{256,320},{320,256},{384,448},{4... | collective-permute-start | bytes 4718600 | tf_op jit(solution)/shard_map/ppermute | solution.py:401
  123.5 8.9 %copy-start.2 = (s32[128,6]{0,1:T(8,128)S(1)}, s32[128,6]{0,1:T(8,128)}, u32[]{:S(2)}) copy-start(s32[128,6]{0,1:T(8,128)} %param.8) | copy-start | bytes 9220
  123.5 8.9 %copy-start.3 = (f32[128,6]{0,1:T(8,128)S(1)}, f32[128,6]{0,1:T(8,128)}, u32[]{:S(2)}) copy-start(f32[128,6]{0,1:T(8,128)} %param.9) | copy-start | bytes 9220
  123.6 13.9 %collective-permute-start.1 = (bf16[1,128,1536]{2,1,0:T(8,128)(2,1)S(1)}, bf16[1,128,1536]{2,1,0:T(8,128)(2,1)S(1)}, u32[]{:S(2)}, u32[]{:S(2)}) collective-permute-start(bf16[1,128,1536]{2,1,0:T(8,128)(2,1)S(1)} %get-tuple-element.27), channel_id=1, source_target_pairs={{0,128},{64,192},{128,256},{192,320},{256,384},{320,448},{384,0},{... | collective-permute-start | bytes 1179656 | tf_op jit(solution)/shard_map/ppermute | solution.py:406
  126.0 15.4 %collective-permute-start.2 = (bf16[1,128,1536]{2,1,0:T(8,128)(2,1)S(1)}, bf16[1,128,1536]{2,1,0:T(8,128)(2,1)S(1)}, u32[]{:S(2)}, u32[]{:S(2)}) collective-permute-start(bf16[1,128,1536]{2,1,0:T(8,128)(2,1)S(1)} %get-tuple-element.26), channel_id=1, source_target_pairs={{0,256},{64,320},{128,384},{192,448},{256,0},{320,64},{384,128},{4... | collective-permute-start | bytes 1179656 | tf_op jit(solution)/shard_map/ppermute | solution.py:406
  130.4 18.3 %collective-permute-start.3 = (bf16[1,128,1536]{2,1,0:T(8,128)(2,1)S(1)}, bf16[1,128,1536]{2,1,0:T(8,128)(2,1)S(1)}, u32[]{:S(2)}, u32[]{:S(2)}) collective-permute-start(bf16[1,128,1536]{2,1,0:T(8,128)(2,1)S(1)} %get-tuple-element.25), channel_id=1, source_target_pairs={{0,384},{64,448},{128,0},{192,64},{256,128},{320,192},{384,256},{4... | collective-permute-start | bytes 1179656 | tf_op jit(solution)/shard_map/ppermute | solution.py:406

commit v3 on v2

--- a/solution.py
+++ b/solution.py
@@ -7,7 +7,6 @@
 
 INTERPRET = False
 PACK_STEPS = 2
-EXPERT_STEP = 32
 F32 = jnp.float32
 BF16 = jnp.bfloat16
 NT = (((1,), (1,)), ((), ()))
@@ -33,7 +32,7 @@
 
 def expert_at(place):
     across, along = place // SIDE, place % SIDE
-    return along * SIDE + (across + along) % SIDE
+    return along * SIDE + (along - across) % SIDE
 
 
 def route_tables(routes, weights, experts):
@@ -161,14 +160,27 @@
     )(routes, weights)
 
 
-def unpack_kernel(plan_ref, back_ref, mixed_ref, grad_ref):
-    token_count, width = mixed_ref.shape
-    piece = 256
-    for at in range(0, width, piece):
-        cols = slice(at, at + piece)
-        total = jnp.dot(plan_ref[...], back_ref[:, cols], preferred_element_type=F32)
-        mixed_ref[:, cols] = (total[:token_count] + total[token_count : 2 * token_count]).astype(BF16)
-        grad_ref[:, cols] = total[2 * token_count :].astype(BF16)
+def unpack_kernel(plan_ref, back_hbm, mixed_ref, grad_ref, back_ref, total_ref, sems):
+    token_count = mixed_ref.shape[0]
+    count = sems.shape[0]
+    block = back_ref.shape[0] // count
+    moves = []
+    for i in range(count):
+        rows = pl.ds(i * block, block)
+        moves.append(pltpu.make_async_copy(back_hbm.at[rows], back_ref.at[rows], sems.at[i]))
+        moves[-1].start()
+    for i in range(count):
+        rows = slice(i * block, (i + 1) * block)
+        moves[i].wait()
+        part = jnp.dot(plan_ref[:, rows], back_ref[rows], preferred_element_type=F32)
+        if i == 0:
+            total_ref[...] = part
+        elif i < count - 1:
+            total_ref[...] += part
+        else:
+            total = total_ref[...] + part
+            mixed_ref[...] = (total[:token_count] + total[token_count : 2 * token_count]).astype(BF16)
+            grad_ref[...] = total[2 * token_count :].astype(BF16)
 
 
 def unpack(plan, back):
@@ -177,16 +189,21 @@
     here = pl.BlockSpec(memory_space=VMEM)
     return pl.pallas_call(
         unpack_kernel,
-        in_specs=[here, here],
+        in_specs=[here, pl.BlockSpec(memory_space=HBM)],
         out_specs=[here, here],
         out_shape=[jax.ShapeDtypeStruct((token_count, width), BF16)] * 2,
+        scratch_shapes=[
+            pltpu.VMEM((rows, width), BF16),
+            pltpu.VMEM((plan.shape[0], width), F32),
+            pltpu.SemaphoreType.DMA((4,)),
+        ],
         compiler_params=pltpu.CompilerParams(vmem_limit_bytes=28 * 1024 * 1024),
         cost_estimate=pl.CostEstimate(
             flops=6 * token_count * rows * width, bytes_accessed=2 * (rows + 5 * token_count) * width, transcendentals=0
         ),
         interpret=INTERPRET,
         name="unpack",
-    )(placed(plan, VMEM), placed(back, VMEM))
+    )(placed(plan, VMEM), placed(back, HBM))
 
 
 def shard_dots(inputs_ref, grads_ref, pair_ref, hidden_ref):
@@ -286,15 +303,14 @@
         grads_ref[head:, cols] = jnp.where(low, roll_half(first), second).reshape(-1, piece).astype(BF16)
 
 
-def sort_slots(inbox, sources, step):
+def sort_slots(inbox):
     rows, width = inbox.shape
     slots = rows // 2
-    part = lambda count: pl.BlockSpec((count, width), lambda i: (i, 0))
+    here = pl.BlockSpec(memory_space=VMEM)
     return pl.pallas_call(
         split_slots,
-        grid=(sources // step,),
-        in_specs=[part(24 * step)],
-        out_specs=[part(12 * step), part(12 * step)],
+        in_specs=[here],
+        out_specs=[here, here],
         out_shape=[jax.ShapeDtypeStruct((slots, width), BF16)] * 2,
         compiler_params=pltpu.CompilerParams(vmem_limit_bytes=28 * 1024 * 1024),
         cost_estimate=pl.CostEstimate(flops=4 * rows * width, bytes_accessed=4 * rows * width, transcendentals=0),
@@ -304,32 +320,38 @@
 
 
 def expert_kernel(
-    sources, inbox_all, gate_ref, up_ref, down_ref, back_ref, pair_ref, hidden_ref, tokens_ref, grads_ref
+    inbox_ref, gate_ref, up_ref, down_ref, back_hbm, pair_hbm, hidden_hbm,
+    tokens_ref, grads_ref, back_ref, pair_ref, hidden_ref, sems,
 ):
-    many = 24 * sources
-    inbox_ref = inbox_all.at[pl.ds(pl.multiple_of(pl.program_id(0) * many, many), many)]
-    width = inbox_ref.shape[1]
+    rows, width = inbox_ref.shape
     ffn = gate_ref.shape[1]
+    sources = rows // 24
     head = 8 * sources
     piece = 256
+    moves = []
+
+    def leave(source, target):
+        moves.append(pltpu.make_async_copy(source, target, sems.at[len(moves)]))
+        moves[-1].start()
+
     split_slots(inbox_ref, tokens_ref, grads_ref)
-    tokens, grads = tokens_ref[...], grads_ref[...]
-    gate_pre = jnp.dot(tokens, gate_ref[...], preferred_element_type=F32)
-    up_pre = jnp.dot(tokens, up_ref[...], preferred_element_type=F32)
-    hidden_grad = lax.dot_general(grads, down_ref[...], NT, preferred_element_type=F32)
-    sigmoid = jax.nn.sigmoid(gate_pre)
-    silu = gate_pre * sigmoid
-    hidden = (silu * up_pre).astype(BF16)
-    up_grad_pre = (hidden_grad * silu).astype(BF16)
-    gate_grad_pre = (hidden_grad * up_pre * sigmoid * (1.0 + gate_pre * (1.0 - sigmoid))).astype(BF16)
-    hidden_ref[...] = hidden
-    pair_ref[:, :ffn] = gate_grad_pre
-    pair_ref[:, ffn:] = up_grad_pre
+    for at in range(0, ffn, piece):
+        cols = slice(at, at + piece)
+        gate_pre = jnp.dot(tokens_ref[...], gate_ref[:, cols], preferred_element_type=F32)
+        up_pre = jnp.dot(tokens_ref[...], up_ref[:, cols], preferred_element_type=F32)
+        hidden_grad = lax.dot_general(grads_ref[...], down_ref[cols, :], NT, preferred_element_type=F32)
+        sigmoid = jax.nn.sigmoid(gate_pre)
+        silu = gate_pre * sigmoid
+        hidden_ref[:, cols] = (silu * up_pre).astype(BF16)
+        pair_ref[:, cols] = (hidden_grad * up_pre * sigmoid * (1.0 + gate_pre * (1.0 - sigmoid))).astype(BF16)
+        pair_ref[:, ffn + at : ffn + at + piece] = (hidden_grad * silu).astype(BF16)
+    leave(hidden_ref, hidden_hbm)
+    leave(pair_ref, pair_hbm)
     for at in range(0, width, piece):
         cols = slice(at, at + piece)
-        outputs = jnp.dot(hidden, down_ref[:, cols], preferred_element_type=F32)
-        slot = lax.dot_general(gate_grad_pre, gate_ref[cols, :], NT, preferred_element_type=F32)
-        slot = slot + lax.dot_general(up_grad_pre, up_ref[cols, :], NT, preferred_element_type=F32)
+        outputs = jnp.dot(hidden_ref[...], down_ref[:, cols], preferred_element_type=F32)
+        slot = lax.dot_general(pair_ref[:, :ffn], gate_ref[cols, :], NT, preferred_element_type=F32)
+        slot = slot + lax.dot_general(pair_ref[:, ffn:], up_ref[cols, :], NT, preferred_element_type=F32)
         out_tail = outputs[head:].reshape(sources // 2, 8, piece)
         slot_tail = slot[head:].reshape(sources // 2, 8, piece)
         low = lax.broadcasted_iota(jnp.int32, out_tail.shape, 1) < 4
@@ -339,31 +361,35 @@
         sent = jnp.concatenate(
             [outputs[:head].reshape(sources, 8, piece), middle, slot[:head].reshape(sources, 8, piece)], axis=1
         )
-        back_ref[:, cols] = sent.reshape(24 * sources, piece).astype(BF16)
-
-
-def run_expert(inbox, gate, up, down, sources, step):
+        back_ref[:, cols] = sent.reshape(rows, piece).astype(BF16)
+        leave(back_ref.at[:, cols], back_hbm.at[:, cols])
+    for move in moves:
+        move.wait()
+
+
+def run_expert(inbox, gate, up, down):
     rows, width = inbox.shape
     ffn = gate.shape[1]
     slots = rows // 2
-    part = lambda count, columns: pl.BlockSpec((count, columns), lambda i: (i, 0))
-    here = pl.BlockSpec(memory_space=VMEM)
-    many, few = 24 * step, 12 * step
-    return pl.pallas_call(
-        lambda *refs: expert_kernel(step, *refs),
-        grid=(sources // step,),
+    here, there = pl.BlockSpec(memory_space=VMEM), pl.BlockSpec(memory_space=HBM)
+    return pl.pallas_call(
+        expert_kernel,
         in_specs=[here, here, here, here],
-        out_specs=[part(many, width), part(few, 2 * ffn), part(few, ffn)],
+        out_specs=[there, there, there],
         out_shape=[
             made((rows, width), BF16, HBM),
             made((slots, 2 * ffn), BF16, HBM),
             made((slots, ffn), BF16, HBM),
         ],
         scratch_shapes=[
-            pltpu.VMEM((few, width), BF16),
-            pltpu.VMEM((few, width), BF16),
+            pltpu.VMEM((slots, width), BF16),
+            pltpu.VMEM((slots, width), BF16),
+            pltpu.VMEM((rows, width), BF16),
+            pltpu.VMEM((slots, 2 * ffn), BF16),
+            pltpu.VMEM((slots, ffn), BF16),
+            pltpu.SemaphoreType.DMA((2 + width // 256,)),
         ],
-        compiler_params=pltpu.CompilerParams(vmem_limit_bytes=28 * 1024 * 1024),
+        compiler_params=pltpu.CompilerParams(vmem_limit_bytes=40 * 1024 * 1024),
         cost_estimate=pl.CostEstimate(
             flops=12 * slots * width * ffn, bytes_accessed=14 * slots * width, transcendentals=slots * ffn
         ),
@@ -388,8 +414,8 @@
     choices, weights = routes.T, route_weights.T
     send = pack(tokens, cotangent, choices, weights, experts, chunk)
     inbox = exchange(send)
-    back, pair_grads, hidden = run_expert(inbox, gate, up, down, experts, EXPERT_STEP)
-    inputs, out_grads = sort_slots(inbox, experts, EXPERT_STEP)
+    back, pair_grads, hidden = run_expert(inbox, gate, up, down)
+    inputs, out_grads = sort_slots(inbox)
     plan = plan_unpack(choices, weights, experts, chunk)
     returned = exchange(back)
     groups = lax.axis_size("dp")

time: 199 us -> 196 us (0.985)
  the two profiles are of different devices: /device:TPU:46 before, /device:TPU:18 now
where the time goes in v3:
time: 196 us
  blocking collectives  91.6 us (47%)
  waiting for transfers between devices  58.9 us (30%)
  Pallas kernels  21.5 us (11%)
  starting transfers between devices  21.3 us (11%)
    all_to_all x1, blocking collectives, exchange(): lax.all_to_all(rows.reshape(experts, chunk, width), 'expert', split_axis=...  91.6 us
    all_to_all x1, waiting for transfers between devices, exchange(): lax.all_to_all(rows.reshape(experts, chunk, width), 'expert', split_axis=...  40.9 us
    ppermute x3, waiting for transfers between devices, shards(): pieces.append(lax.ppermute(mine[step:step + 1], 'dp', hop))  14.7 us
    ppermute x3, starting transfers between devices, shards(): pieces.append(lax.ppermute(mine[step:step + 1], 'dp', hop))  10.6 us
    all_to_all x1, starting transfers between devices, exchange(): lax.all_to_all(rows.reshape(experts, chunk, width), 'expert', split_axis=...  8.83 us
    pallas_call x1, Pallas kernels, run_expert(): pl.pallas_call(expert_kernel, in_specs=[here, here, here, here], out_spec...  6.76 us
    pallas_call x2, Pallas kernels, weight_half(): pl.pallas_call(lambda *refs: weight_kernel(arrived is None, *refs), grid_...  6.3 us
  transfers between devices with their start and end apart: 5, of which 5 were waited for; matrix products, arithmetic and copies ran while one was open for 0% of the time, Pallas kernels for 4%

profile of v3, /device:TPU:18, one launch (start us, length us, event | category | flops | bytes accessed | tf_op | source)
XLA Modules:
  0.0 195.5 jit_solution(2298691131313002559)
XLA Ops:
  0.6 2.3 %pack.1 = bf16[1536,1024]{1,0:T(8,128)(2,1)S(1)} custom-call(s32[6,128]{1,0:T(8,128)} %bitcast.15, f32[6,128]{1,0:T(8,128)} %bitcast.17, bf16[128,1024]{1,0:T(8,128)(2,1)} %refs_2_.1, bf16[128,1024]{1,0:T(8,128)(2,1)} %refs_3_.1), custom_call_target="tpu_custom_call" | custom-call | flops 805306368 | bytes 3670016 | tf_op jit(solution)/shard_map/pack/pallas_call | solution.py:103
  2.9 0.0 copy-start.4
  2.9 0.0 copy-start.5
  3.0 0.0 copy-start.6
  3.0 91.6 %all_to_all.10 = bf16[64,24,1024]{2,1,0:T(8,128)(2,1)S(1)} all-to-all(bf16[64,24,1024]{2,1,0:T(8,128)(2,1)S(1)} %bitcast.14), channel_id=1, replica_groups={{0,9,18,27,36,45,54,63,7,8,17,26,35,44,53,62,6,15,16,25,34,43,52,61,5,1..., dimensions={0} | all-to-all | bytes 6291456 | tf_op jit(solution)/shard_map/all_to_all | solution.py:411
  94.5 0.0 copy-done.4
  94.6 0.0 copy-done.5
  94.6 0.0 copy-done.6
  94.6 6.8 %expert.1 = (bf16[1536,1024]{1,0:T(8,128)(2,1)}, bf16[768,1024]{1,0:T(8,128)(2,1)}, bf16[768,512]{1,0:T(8,128)(2,1)}) custom-call(bf16[1536,1024]{1,0:T(8,128)(2,1)S(1)} %bitcast.12, bf16[1024,512]{1,0:T(8,128)(2,1)S(1)} %bitcast.19, bf16[1024,512]{1,0:T(8,128)(2,1)S(1)} %bitcast.20, bf16[512,1024]{1,0:T(8,128)(2,1)S(1)} %bitcast.21), custom_call_target="tpu_custom_call" | custom-call | flops 4831838208 | bytes 11010048 | tf_op jit(solution)/shard_map/expert/pallas_call | solution.py:375
  101.3 8.8 %all-to-all-start.1 = ((bf16[64,24,1024]{2,1,0:T(8,128)(2,1)}), bf16[64,24,1024]{2,1,0:T(8,128)(2,1)}, u32[]{:S(2)}, u32[]{:S(2)}) async-start(bf16[64,24,1024]{2,1,0:T(8,128)(2,1)} %bitcast.22), calls=%async_computation.1 | async-start | bytes 6291456 | tf_op jit(solution)/shard_map/all_to_all | solution.py:411
  110.2 0.1 pad_add_fusion.1.refs_0_
  110.3 0.5 sort_slots.1
  110.8 0.9 copy-done
  111.7 0.2 copy-done.1
  111.9 3.1 %weight_half.2 = bf16[4,128,1536]{2,1,0:T(8,128)(2,1)S(1)} custom-call(s32[2]{0:T(128)S(1)} %pad_add_fusion.1.refs_0_, bf16[768,1024]{1,0:T(8,128)(2,1)S(1)} %get-tuple-element.18.refs_1_, bf16[768,1024]{1,0:T(8,128)(2,1)S(1)} %get-tuple-element.19.refs_2_, bf16[768,1024]{1,0:T(8,128)(2,1)S(1)} %copy-done, bf16[768,512]{1,0:T(8,128)(2,1)S(1)} %copy-done.1), custom_call_target="tpu_custom_call" | custom-call | flops 1207959552 | bytes 5505024 | tf_op jit(solution)/shard_map/weight_half/pallas_call | solution.py:235
  115.0 1.9 collective-permute-start
  116.9 0.1 pad_add_fusion.refs_0_
  117.0 3.3 %collective-permute-done.refs_5_ = bf16[4,128,1536]{2,1,0:T(8,128)(2,1)S(1)} collective-permute-done((bf16[4,128,1536]{2,1,0:T(8,128)(2,1)S(1)}, bf16[4,128,1536]{2,1,0:T(8,128)(2,1)S(1)}, u32[]{:S(2)}, u32[]{:S(2)}) %collective-permute-start) | collective-permute-done | bytes 1572896 | tf_op jit(solution)/shard_map/ppermute | solution.py:427
  120.3 3.2 %weight_half.3 = bf16[4,128,1536]{2,1,0:T(8,128)(2,1)S(1)} custom-call(s32[2]{0:T(128)S(1)} %pad_add_fusion.refs_0_, bf16[768,1024]{1,0:T(8,128)(2,1)S(1)} %get-tuple-element.18.refs_1_, bf16[768,1024]{1,0:T(8,128)(2,1)S(1)} %get-tuple-element.19.refs_2_, bf16[768,1024]{1,0:T(8,128)(2,1)S(1)} %copy-done, bf16[768,512]{1,0:T(8,128)(2,1)S(1)} %copy-done.1, ...), custom_call_target="tpu_custom_call" | custom-call | flops 1207959552 | bytes 5505024 | tf_op jit(solution)/shard_map/weight_half/pallas_call | solution.py:235
  123.5 0.0 copy-start.2
  123.5 0.0 copy-start.3
  123.5 0.1 fusion
  123.6 3.4 %collective-permute-start.1 = (bf16[1,128,1536]{2,1,0:T(8,128)(2,1)S(1)}, bf16[1,128,1536]{2,1,0:T(8,128)(2,1)S(1)}, u32[]{:S(2)}, u32[]{:S(2)}) collective-permute-start(bf16[1,128,1536]{2,1,0:T(8,128)(2,1)S(1)} %get-tuple-element.27), channel_id=1, source_target_pairs={{0,128},{64,192},{128,256},{192,320},{256,384},{320,448},{384,0},{... | collective-permute-start | bytes 1179656 | tf_op jit(solution)/shard_map/ppermute | solution.py:432
  127.0 3.0 %collective-permute-start.2 = (bf16[1,128,1536]{2,1,0:T(8,128)(2,1)S(1)}, bf16[1,128,1536]{2,1,0:T(8,128)(2,1)S(1)}, u32[]{:S(2)}, u32[]{:S(2)}) collective-permute-start(bf16[1,128,1536]{2,1,0:T(8,128)(2,1)S(1)} %get-tuple-element.26), channel_id=1, source_target_pairs={{0,256},{64,320},{128,384},{192,448},{256,0},{320,64},{384,128},{4... | collective-permute-start | bytes 1179656 | tf_op jit(solution)/shard_map/ppermute | solution.py:432
  130.1 4.1 %collective-permute-start.3 = (bf16[1,128,1536]{2,1,0:T(8,128)(2,1)S(1)}, bf16[1,128,1536]{2,1,0:T(8,128)(2,1)S(1)}, u32[]{:S(2)}, u32[]{:S(2)}) collective-permute-start(bf16[1,128,1536]{2,1,0:T(8,128)(2,1)S(1)} %get-tuple-element.25), channel_id=1, source_target_pairs={{0,384},{64,448},{128,0},{192,64},{256,128},{320,192},{384,256},{4... | collective-permute-start | bytes 1179656 | tf_op jit(solution)/shard_map/ppermute | solution.py:432
  134.2 0.7 plan.1.plan_ref
  135.0 2.5 %collective-permute-done.1.refs_1_ = bf16[1,128,1536]{2,1,0:T(8,128)(2,1)S(1)} collective-permute-done((bf16[1,128,1536]{2,1,0:T(8,128)(2,1)S(1)}, bf16[1,128,1536]{2,1,0:T(8,128)(2,1)S(1)}, u32[]{:S(2)}, u32[]{:S(2)}) %collective-permute-start.1) | collective-permute-done | bytes 393248 | tf_op jit(solution)/shard_map/ppermute | solution.py:432
  137.5 5.0 %collective-permute-done.2.refs_2_ = bf16[1,128,1536]{2,1,0:T(8,128)(2,1)S(1)} collective-permute-done((bf16[1,128,1536]{2,1,0:T(8,128)(2,1)S(1)}, bf16[1,128,1536]{2,1,0:T(8,128)(2,1)S(1)}, u32[]{:S(2)}, u32[]{:S(2)}) %collective-permute-start.2) | collective-permute-done | bytes 393248 | tf_op jit(solution)/shard_map/ppermute | solution.py:432
  142.5 7.3 %collective-permute-done.3.refs_3_ = bf16[1,128,1536]{2,1,0:T(8,128)(2,1)S(1)} collective-permute-done((bf16[1,128,1536]{2,1,0:T(8,128)(2,1)S(1)}, bf16[1,128,1536]{2,1,0:T(8,128)(2,1)S(1)}, u32[]{:S(2)}, u32[]{:S(2)}) %collective-permute-start.3) | collective-permute-done | bytes 393248 | tf_op jit(solution)/shard_map/ppermute | solution.py:432
  149.7 1.0 finish.1
  150.7 40.9 %all-to-all-done.1 = bf16[64,24,1024]{2,1,0:T(8,128)(2,1)} async-done(((bf16[64,24,1024]{2,1,0:T(8,128)(2,1)}), bf16[64,24,1024]{2,1,0:T(8,128)(2,1)}, u32[]{:S(2)}, u32[]{:S(2)}) %all-to-all-start.1) | async-done | bytes 3145760 | tf_op jit(solution)/shard_map/all_to_all | solution.py:411
  191.7 3.9 %unpack.1 = (bf16[128,1024]{1,0:T(8,128)(2,1)}, bf16[128,1024]{1,0:T(8,128)(2,1)}) custom-call(bf16[384,1536]{1,0:T(8,128)(2,1)S(1)} %plan.1.plan_ref, bf16[1536,1024]{1,0:T(8,128)(2,1)} %bitcast.8.back_hbm), custom_call_target="tpu_custom_call" | custom-call | flops 1207959552 | bytes 4456448 | tf_op jit(solution)/shard_map/unpack/pallas_call | solution.py:190
  (4 shorter events, 0.0 us)
Async XLA Ops:
  2.9 91.6 %copy-start.4 = (bf16[1,1024,512]{2,1,0:T(8,128)(2,1)S(1)}, bf16[1,1024,512]{2,1,0:T(8,128)(2,1)}, u32[]{:S(2)}) copy-start(bf16[1,1024,512]{2,1,0:T(8,128)(2,1)} %param.10) | copy-start | bytes 3145732
  2.9 91.6 %copy-start.5 = (bf16[1,1024,512]{2,1,0:T(8,128)(2,1)S(1)}, bf16[1,1024,512]{2,1,0:T(8,128)(2,1)}, u32[]{:S(2)}) copy-start(bf16[1,1024,512]{2,1,0:T(8,128)(2,1)} %param.11) | copy-start | bytes 3145732
  3.0 91.6 %copy-start.6 = (bf16[1,512,1024]{2,1,0:T(8,128)(2,1)S(1)}, bf16[1,512,1024]{2,1,0:T(8,128)(2,1)}, u32[]{:S(2)}) copy-start(bf16[1,512,1024]{2,1,0:T(8,128)(2,1)} %param.12) | copy-start | bytes 3145732
  101.3 90.3 %all-to-all-start.1 = ((bf16[64,24,1024]{2,1,0:T(8,128)(2,1)}), bf16[64,24,1024]{2,1,0:T(8,128)(2,1)}, u32[]{:S(2)}, u32[]{:S(2)}) async-start(bf16[64,24,1024]{2,1,0:T(8,128)(2,1)} %bitcast.22), calls=%async_computation.1 | async-start | bytes 6291456 | tf_op jit(solution)/shard_map/all_to_all | solution.py:411
  110.3 1.4 copy-start
  110.3 1.6 copy-start.1
  115.0 5.3 %collective-permute-start = (bf16[4,128,1536]{2,1,0:T(8,128)(2,1)S(1)}, bf16[4,128,1536]{2,1,0:T(8,128)(2,1)S(1)}, u32[]{:S(2)}, u32[]{:S(2)}) collective-permute-start(bf16[4,128,1536]{2,1,0:T(8,128)(2,1)S(1)} %weight_half.2), channel_id=1, source_target_pairs={{0,64},{64,0},{128,192},{192,128},{256,320},{320,256},{384,448},{4... | collective-permute-start | bytes 4718600 | tf_op jit(solution)/shard_map/ppermute | solution.py:427
  123.5 10.7 %copy-start.2 = (s32[128,6]{0,1:T(8,128)S(1)}, s32[128,6]{0,1:T(8,128)}, u32[]{:S(2)}) copy-start(s32[128,6]{0,1:T(8,128)} %param.8) | copy-start | bytes 9220
  123.5 10.7 %copy-start.3 = (f32[128,6]{0,1:T(8,128)S(1)}, f32[128,6]{0,1:T(8,128)}, u32[]{:S(2)}) copy-start(f32[128,6]{0,1:T(8,128)} %param.9) | copy-start | bytes 9220
  123.6 13.9 %collective-permute-start.1 = (bf16[1,128,1536]{2,1,0:T(8,128)(2,1)S(1)}, bf16[1,128,1536]{2,1,0:T(8,128)(2,1)S(1)}, u32[]{:S(2)}, u32[]{:S(2)}) collective-permute-start(bf16[1,128,1536]{2,1,0:T(8,128)(2,1)S(1)} %get-tuple-element.27), channel_id=1, source_target_pairs={{0,128},{64,192},{128,256},{192,320},{256,384},{320,448},{384,0},{... | collective-permute-start | bytes 1179656 | tf_op jit(solution)/shard_map/ppermute | solution.py:432
  127.0 15.4 %collective-permute-start.2 = (bf16[1,128,1536]{2,1,0:T(8,128)(2,1)S(1)}, bf16[1,128,1536]{2,1,0:T(8,128)(2,1)S(1)}, u32[]{:S(2)}, u32[]{:S(2)}) collective-permute-start(bf16[1,128,1536]{2,1,0:T(8,128)(2,1)S(1)} %get-tuple-element.26), channel_id=1, source_target_pairs={{0,256},{64,320},{128,384},{192,448},{256,0},{320,64},{384,128},{4... | collective-permute-start | bytes 1179656 | tf_op jit(solution)/shard_map/ppermute | solution.py:432
  130.1 19.6 %collective-permute-start.3 = (bf16[1,128,1536]{2,1,0:T(8,128)(2,1)S(1)}, bf16[1,128,1536]{2,1,0:T(8,128)(2,1)S(1)}, u32[]{:S(2)}, u32[]{:S(2)}) collective-permute-start(bf16[1,128,1536]{2,1,0:T(8,128)(2,1)S(1)} %get-tuple-element.25), channel_id=1, source_target_pairs={{0,384},{64,448},{128,0},{192,64},{256,128},{320,192},{384,256},{4... | collective-permute-start | bytes 1179656 | tf_op jit(solution)/shard_map/ppermute | solution.py:432

commit v4 on v3

--- a/solution.py
+++ b/solution.py
@@ -6,7 +6,7 @@
 from jax.sharding import PartitionSpec as P
 
 INTERPRET = False
-PACK_STEPS = 2
+PIECES = 4
 F32 = jnp.float32
 BF16 = jnp.bfloat16
 NT = (((1,), (1,)), ((), ()))
@@ -32,7 +32,7 @@
 
 def expert_at(place):
     across, along = place // SIDE, place % SIDE
-    return along * SIDE + (along - across) % SIDE
+    return (across + 4 * along) % SIDE * SIDE + along
 
 
 def route_tables(routes, weights, experts):
@@ -52,69 +52,62 @@
 
 
 def pack_kernel(
-    chunk, routes_hbm, weights_hbm, tokens_hbm, cot_hbm, send_ref, routes, weights, rows, rank_ref, weight_ref, sems
+    experts, chunk, routes_hbm, weights_hbm, tokens_hbm, cot_hbm, send_ref, routes, weights, rows, sems
 ):
     token_count = routes.shape[1]
-    total = rank_ref.shape[0]
-    experts = send_ref.shape[0] // chunk
-    step = pl.program_id(0)
-
-    @pl.when(step == 0)
-    def _():
-        moves = [
-            pltpu.make_async_copy(source, target, sems.at[i])
-            for i, (source, target) in enumerate(
-                [
-                    (routes_hbm, routes),
-                    (weights_hbm, weights),
-                    (tokens_hbm, rows.at[pl.ds(0, token_count)]),
-                    (cot_hbm, rows.at[pl.ds(token_count, token_count)]),
-                ]
-            )
-        ]
-        for move in moves:
-            move.start()
-        moves[0].wait()
-        moves[1].wait()
-        rank_ref[...], weight_ref[...] = route_tables(routes[...], weights[...], total)
-        moves[2].wait()
-        moves[3].wait()
-
-    here = pl.ds(pl.multiple_of(step * experts, experts), experts)
-    full = (experts, chunk, token_count)
+    moves = [
+        pltpu.make_async_copy(source, target, sems.at[i])
+        for i, (source, target) in enumerate(
+            [
+                (routes_hbm, routes),
+                (weights_hbm, weights),
+                (tokens_hbm, rows.at[pl.ds(0, token_count)]),
+                (cot_hbm, rows.at[pl.ds(token_count, token_count)]),
+            ]
+        )
+    ]
+    for move in moves:
+        move.start()
+    moves[0].wait()
+    moves[1].wait()
+    rank, weight = route_tables(routes[...], weights[...], experts)
+    group = experts // 4
+    full = (group, chunk, token_count)
     slot, backward = chunk_slot(lax.broadcasted_iota(jnp.int32, full, 1))
-    hit = jnp.broadcast_to(rank_ref[here][:, None, :], full) == slot
-    one = jnp.where(hit, 1.0, 0.0)
-    forward_pick = jnp.where(backward, 0.0, one).reshape(experts * chunk, token_count).astype(BF16)
-    backward_pick = jnp.where(backward, one, 0.0).reshape(experts * chunk, token_count).astype(BF16)
-    chosen = jnp.where(hit, jnp.broadcast_to(weight_ref[here][:, None, :], full), 0.0)
-    scale = jnp.where(backward, jnp.sum(chosen, axis=2, keepdims=True), 1.0).reshape(experts * chunk, token_count)
-    pick = jnp.concatenate([forward_pick, backward_pick], axis=1)
-    picked = jnp.dot(pick, rows[...], preferred_element_type=F32)
-    for at in range(0, picked.shape[1], token_count):
-        send_ref[:, at : at + token_count] = (picked[:, at : at + token_count] * scale).astype(BF16)
+    for at in range(0, experts, group):
+        hit = jnp.broadcast_to(rank[at : at + group][:, None, :], full) == slot
+        one = jnp.where(hit, 1.0, 0.0)
+        forward_pick = jnp.where(backward, 0.0, one).reshape(group * chunk, token_count).astype(BF16)
+        backward_pick = jnp.where(backward, one, 0.0).reshape(group * chunk, token_count).astype(BF16)
+        chosen = jnp.where(hit, jnp.broadcast_to(weight[at : at + group][:, None, :], full), 0.0)
+        scale = jnp.where(backward, jnp.sum(chosen, axis=2, keepdims=True), 1.0).reshape(group * chunk, token_count)
+        pick = jnp.concatenate([forward_pick, backward_pick], axis=1)
+        if at == 0:
+            moves[2].wait()
+            moves[3].wait()
+        picked = jnp.dot(pick, rows[...], preferred_element_type=F32)
+        here = slice(at * chunk, (at + group) * chunk)
+        for col in range(0, picked.shape[1], token_count):
+            cols = slice(col, col + token_count)
+            send_ref[here, cols] = (picked[:, cols] * scale).astype(BF16)
 
 
 def pack(tokens, cotangent, routes, weights, experts, chunk):
     token_count, width = tokens.shape
     rows = experts * chunk
-    steps = PACK_STEPS
-    hbm = pl.BlockSpec(memory_space=pltpu.MemorySpace.HBM)
-    return pl.pallas_call(
-        lambda *refs: pack_kernel(chunk, *refs),
-        grid=(steps,),
+    hbm = pl.BlockSpec(memory_space=HBM)
+    return pl.pallas_call(
+        lambda *refs: pack_kernel(experts, chunk, *refs),
         in_specs=[hbm, hbm, hbm, hbm],
-        out_specs=pl.BlockSpec((rows // steps, width), lambda i: (i, 0)),
-        out_shape=jax.ShapeDtypeStruct((rows, width), BF16),
+        out_specs=pl.BlockSpec(memory_space=VMEM),
+        out_shape=made((rows, width), BF16, VMEM),
         scratch_shapes=[
             pltpu.VMEM(routes.shape, jnp.int32),
             pltpu.VMEM(weights.shape, F32),
             pltpu.VMEM((2 * token_count, width), BF16),
-            pltpu.VMEM((experts, token_count), F32),
-            pltpu.VMEM((experts, token_count), F32),
             pltpu.SemaphoreType.DMA((4,)),
         ],
-        compiler_params=pltpu.CompilerParams(vmem_limit_bytes=28 * 1024 * 1024),
+        compiler_params=pltpu.CompilerParams(vmem_limit_bytes=14 * 1024 * 1024),
         cost_estimate=pl.CostEstimate(
             flops=4 * rows * token_count * width, bytes_accessed=2 * (rows + 2 * token_count) * width, transcendentals=0
         ),
@@ -140,9 +133,12 @@
     slot, backward = chunk_slot(row)
     hit = widen(rank) == slot
     ahead = jnp.where(backward, 0.0, jnp.where(hit, 1.0, 0.0))
-    plan_ref[:token_count, :] = (widen(coarse) * ahead).astype(BF16)
-    plan_ref[token_count : 2 * token_count, :] = (widen(weight - coarse) * ahead).astype(BF16)
-    plan_ref[2 * token_count :, :] = jnp.where(backward & hit, 1.0, 0.0).astype(BF16)
+    parts = [widen(coarse) * ahead, widen(weight - coarse) * ahead, jnp.where(backward & hit, 1.0, 0.0)]
+    block = plan_ref.shape[1]
+    for i, part in enumerate(parts):
+        for at in range(0, rows, block):
+            first = 3 * token_count * (at // block) + i * token_count
+            plan_ref[first : first + token_count, :] = part[:, at : at + block].astype(BF16)
 
 
 def plan_unpack(routes, weights, experts, chunk):
@@ -150,8 +146,8 @@
     rows = experts * chunk
     return pl.pallas_call(
         lambda *refs: plan_kernel(experts, chunk, *refs),
-        out_shape=jax.ShapeDtypeStruct((3 * token_count, rows), BF16),
-        compiler_params=pltpu.CompilerParams(vmem_limit_bytes=28 * 1024 * 1024),
+        out_shape=made((3 * token_count * PIECES, rows // PIECES), BF16, HBM),
+        compiler_params=pltpu.CompilerParams(vmem_limit_bytes=14 * 1024 * 1024),
         cost_estimate=pl.CostEstimate(
             flops=6 * token_count * rows * experts, bytes_accessed=6 * token_count * rows, transcendentals=0
         ),
@@ -160,22 +156,22 @@
     )(routes, weights)
 
 
-def unpack_kernel(plan_ref, back_hbm, mixed_ref, grad_ref, back_ref, total_ref, sems):
+def unpack_kernel(plan_hbm, back_ref, mixed_ref, grad_ref, plan_ref, total_ref, sems):
     token_count = mixed_ref.shape[0]
-    count = sems.shape[0]
-    block = back_ref.shape[0] // count
+    block = back_ref.shape[0] // PIECES
+    deep = 3 * token_count
     moves = []
-    for i in range(count):
-        rows = pl.ds(i * block, block)
-        moves.append(pltpu.make_async_copy(back_hbm.at[rows], back_ref.at[rows], sems.at[i]))
+    for i in range(PIECES):
+        rows = pl.ds(i * deep, deep)
+        moves.append(pltpu.make_async_copy(plan_hbm.at[rows], plan_ref.at[rows], sems.at[i]))
         moves[-1].start()
-    for i in range(count):
-        rows = slice(i * block, (i + 1) * block)
+    for i in range(PIECES):
         moves[i].wait()
-        part = jnp.dot(plan_ref[:, rows], back_ref[rows], preferred_element_type=F32)
+        chosen = plan_ref[i * deep : (i + 1) * deep]
+        part = jnp.dot(chosen, back_ref[i * block : (i + 1) * block], preferred_element_type=F32)
         if i == 0:
             total_ref[...] = part
-        elif i < count - 1:
+        elif i < PIECES - 1:
             total_ref[...] += part
         else:
             total = total_ref[...] + part
@@ -184,26 +180,26 @@
 
 
 def unpack(plan, back):
-    token_count = plan.shape[0] // 3
+    token_count = plan.shape[0] // (3 * PIECES)
     rows, width = back.shape
     here = pl.BlockSpec(memory_space=VMEM)
     return pl.pallas_call(
         unpack_kernel,
-        in_specs=[here, pl.BlockSpec(memory_space=HBM)],
+        in_specs=[pl.BlockSpec(memory_space=HBM), here],
         out_specs=[here, here],
         out_shape=[jax.ShapeDtypeStruct((token_count, width), BF16)] * 2,
         scratch_shapes=[
-            pltpu.VMEM((rows, width), BF16),
-            pltpu.VMEM((plan.shape[0], width), F32),
-            pltpu.SemaphoreType.DMA((4,)),
+            pltpu.VMEM(plan.shape, BF16),
+            pltpu.VMEM((3 * token_count, width), F32),
+            pltpu.SemaphoreType.DMA((PIECES,)),
         ],
-        compiler_params=pltpu.CompilerParams(vmem_limit_bytes=28 * 1024 * 1024),
+        compiler_params=pltpu.CompilerParams(vmem_limit_bytes=14 * 1024 * 1024),
         cost_estimate=pl.CostEstimate(
             flops=6 * token_count * rows * width, bytes_accessed=2 * (rows + 5 * token_count) * width, transcendentals=0
         ),
         interpret=INTERPRET,
         name="unpack",
-    )(placed(plan, VMEM), placed(back, HBM))
+    )(placed(plan, HBM), back)
 
 
 def shard_dots(inputs_ref, grads_ref, pair_ref, hidden_ref):
@@ -241,7 +237,7 @@
             out_specs=part,
         ),
         out_shape=jax.ShapeDtypeStruct((chips, depth, columns), BF16),
-        compiler_params=pltpu.CompilerParams(vmem_limit_bytes=28 * 1024 * 1024),
+        compiler_params=pltpu.CompilerParams(vmem_limit_bytes=14 * 1024 * 1024),
         cost_estimate=pl.CostEstimate(
             flops=slots * width * columns, bytes_accessed=2 * (slots + width) * columns, transcendentals=0
         ),
@@ -273,7 +269,7 @@
             jax.ShapeDtypeStruct((1, depth, ffn), F32),
             jax.ShapeDtypeStruct((1, ffn, depth), F32),
         ],
-        compiler_params=pltpu.CompilerParams(vmem_limit_bytes=28 * 1024 * 1024),
+        compiler_params=pltpu.CompilerParams(vmem_limit_bytes=14 * 1024 * 1024),
         cost_estimate=pl.CostEstimate(
             flops=4 * depth * columns, bytes_accessed=12 * depth * columns, transcendentals=0
         ),
@@ -303,38 +299,9 @@
         grads_ref[head:, cols] = jnp.where(low, roll_half(first), second).reshape(-1, piece).astype(BF16)
 
 
-def sort_slots(inbox):
-    rows, width = inbox.shape
-    slots = rows // 2
-    here = pl.BlockSpec(memory_space=VMEM)
-    return pl.pallas_call(
-        split_slots,
-        in_specs=[here],
-        out_specs=[here, here],
-        out_shape=[jax.ShapeDtypeStruct((slots, width), BF16)] * 2,
-        compiler_params=pltpu.CompilerParams(vmem_limit_bytes=28 * 1024 * 1024),
-        cost_estimate=pl.CostEstimate(flops=4 * rows * width, bytes_accessed=4 * rows * width, transcendentals=0),
-        interpret=INTERPRET,
-        name="sort_slots",
-    )(inbox)
-
-
-def expert_kernel(
-    inbox_ref, gate_ref, up_ref, down_ref, back_hbm, pair_hbm, hidden_hbm,
-    tokens_ref, grads_ref, back_ref, pair_ref, hidden_ref, sems,
-):
-    rows, width = inbox_ref.shape
+def hidden_parts(gate_ref, up_ref, down_ref, tokens_ref, grads_ref, pair_ref, hidden_ref):
     ffn = gate_ref.shape[1]
-    sources = rows // 24
-    head = 8 * sources
     piece = 256
-    moves = []
-
-    def leave(source, target):
-        moves.append(pltpu.make_async_copy(source, target, sems.at[len(moves)]))
-        moves[-1].start()
-
-    split_slots(inbox_ref, tokens_ref, grads_ref)
     for at in range(0, ffn, piece):
         cols = slice(at, at + piece)
         gate_pre = jnp.dot(tokens_ref[...], gate_ref[:, cols], preferred_element_type=F32)
@@ -345,24 +312,83 @@
         hidden_ref[:, cols] = (silu * up_pre).astype(BF16)
         pair_ref[:, cols] = (hidden_grad * up_pre * sigmoid * (1.0 + gate_pre * (1.0 - sigmoid))).astype(BF16)
         pair_ref[:, ffn + at : ffn + at + piece] = (hidden_grad * silu).astype(BF16)
-    leave(hidden_ref, hidden_hbm)
-    leave(pair_ref, pair_hbm)
-    for at in range(0, width, piece):
-        cols = slice(at, at + piece)
-        outputs = jnp.dot(hidden_ref[...], down_ref[:, cols], preferred_element_type=F32)
-        slot = lax.dot_general(pair_ref[:, :ffn], gate_ref[cols, :], NT, preferred_element_type=F32)
-        slot = slot + lax.dot_general(pair_ref[:, ffn:], up_ref[cols, :], NT, preferred_element_type=F32)
-        out_tail = outputs[head:].reshape(sources // 2, 8, piece)
-        slot_tail = slot[head:].reshape(sources // 2, 8, piece)
-        low = lax.broadcasted_iota(jnp.int32, out_tail.shape, 1) < 4
-        first = jnp.where(low, out_tail, roll_half(slot_tail))
-        second = jnp.where(low, roll_half(out_tail), slot_tail)
-        middle = jnp.concatenate([first[:, None], second[:, None]], axis=1).reshape(sources, 8, piece)
-        sent = jnp.concatenate(
-            [outputs[:head].reshape(sources, 8, piece), middle, slot[:head].reshape(sources, 8, piece)], axis=1
-        )
-        back_ref[:, cols] = sent.reshape(rows, piece).astype(BF16)
-        leave(back_ref.at[:, cols], back_hbm.at[:, cols])
+
+
+def again_kernel(inbox_ref, gate_ref, up_ref, down_ref, tokens_ref, grads_ref, pair_ref, hidden_ref):
+    split_slots(inbox_ref, tokens_ref, grads_ref)
+    hidden_parts(gate_ref, up_ref, down_ref, tokens_ref, grads_ref, pair_ref, hidden_ref)
+
+
+def parts_again(inbox, gate, up, down):
+    rows, width = inbox.shape
+    ffn = gate.shape[1]
+    slots = rows // 2
+    here = pl.BlockSpec(memory_space=VMEM)
+    return pl.pallas_call(
+        again_kernel,
+        in_specs=[here, here, here, here],
+        out_specs=[here, here, here, here],
+        out_shape=[
+            jax.ShapeDtypeStruct((slots, width), BF16),
+            jax.ShapeDtypeStruct((slots, width), BF16),
+            jax.ShapeDtypeStruct((slots, 2 * ffn), BF16),
+            jax.ShapeDtypeStruct((slots, ffn), BF16),
+        ],
+        compiler_params=pltpu.CompilerParams(vmem_limit_bytes=14 * 1024 * 1024),
+        cost_estimate=pl.CostEstimate(
+            flops=6 * slots * width * ffn, bytes_accessed=12 * slots * width, transcendentals=slots * ffn
+        ),
+        interpret=INTERPRET,
+        name="parts_again",
+    )(inbox, gate, up, down)
+
+
+def expert_kernel(
+    inbox_ref, gate_ref, up_ref, down_ref, back_hbm,
+    tokens_ref, grads_ref, back_ref, pair_ref, hidden_ref, sems,
+):
+    rows, width = inbox_ref.shape
+    ffn = gate_ref.shape[1]
+    sources = rows // 24
+    head = 8 * sources
+    piece = 256
+    moves = []
+
+    def leave(source, target):
+        moves.append(pltpu.make_async_copy(source, target, sems.at[len(moves)]))
+        moves[-1].start()
+
+    split_slots(inbox_ref, tokens_ref, grads_ref)
+    hidden_parts(gate_ref, up_ref, down_ref, tokens_ref, grads_ref, pair_ref, hidden_ref)
+    half = sources // 2
+    for start in range(0, sources, half):
+        mine = [
+            slice(8 * start, 8 * (start + half)),
+            slice(head + 4 * start, head + 4 * (start + half)),
+        ]
+
+        def some(ref, cols):
+            return jnp.concatenate([ref[rows, cols] for rows in mine], axis=0)
+
+        hidden = some(hidden_ref, slice(None))
+        gate_grad_pre, up_grad_pre = some(pair_ref, slice(0, ffn)), some(pair_ref, slice(ffn, 2 * ffn))
+        here = slice(24 * start, 24 * (start + half))
+        for at in range(0, width, piece):
+            cols = slice(at, at + piece)
+            outputs = jnp.dot(hidden, down_ref[:, cols], preferred_element_type=F32)
+            slot = lax.dot_general(gate_grad_pre, gate_ref[cols, :], NT, preferred_element_type=F32)
+            slot = slot + lax.dot_general(up_grad_pre, up_ref[cols, :], NT, preferred_element_type=F32)
+            out_tail = outputs[8 * half :].reshape(half // 2, 8, piece)
+            slot_tail = slot[8 * half :].reshape(half // 2, 8, piece)
+            low = lax.broadcasted_iota(jnp.int32, out_tail.shape, 1) < 4
+            first = jnp.where(low, out_tail, roll_half(slot_tail))
+            second = jnp.where(low, roll_half(out_tail), slot_tail)
+            middle = jnp.concatenate([first[:, None], second[:, None]], axis=1).reshape(half, 8, piece)
+            sent = jnp.concatenate(
+                [outputs[: 8 * half].reshape(half, 8, piece), middle, slot[: 8 * half].reshape(half, 8, piece)], axis=1
+            )
+            back_ref[here, cols] = sent.reshape(24 * half, piece).astype(BF16)
+        leave(back_ref.at[here], back_hbm.at[here])
     for move in moves:
         move.wait()
 
@@ -375,19 +401,15 @@
     return pl.pallas_call(
         expert_kernel,
         in_specs=[here, here, here, here],
-        out_specs=[there, there, there],
-        out_shape=[
-            made((rows, width), BF16, HBM),
-            made((slots, 2 * ffn), BF16, HBM),
-            made((slots, ffn), BF16, HBM),
-        ],
+        out_specs=there,
+        out_shape=made((rows, width), BF16, HBM),
         scratch_shapes=[
             pltpu.VMEM((slots, width), BF16),
             pltpu.VMEM((slots, width), BF16),
             pltpu.VMEM((rows, width), BF16),
             pltpu.VMEM((slots, 2 * ffn), BF16),
             pltpu.VMEM((slots, ffn), BF16),
-            pltpu.SemaphoreType.DMA((2 + width // 256,)),
+            pltpu.SemaphoreType.DMA((2,)),
         ],
         compiler_params=pltpu.CompilerParams(vmem_limit_bytes=40 * 1024 * 1024),
         cost_estimate=pl.CostEstimate(
@@ -414,8 +436,8 @@
     choices, weights = routes.T, route_weights.T
     send = pack(tokens, cotangent, choices, weights, experts, chunk)
     inbox = exchange(send)
-    back, pair_grads, hidden = run_expert(inbox, gate, up, down)
-    inputs, out_grads = sort_slots(inbox)
+    back = run_expert(inbox, gate, up, down)
+    inputs, out_grads, pair_grads, hidden = parts_again(inbox, gate, up, down)
     plan = plan_unpack(choices, weights, experts, chunk)
     returned = exchange(back)
     groups = lax.axis_size("dp")

time: 196 us -> 189 us (0.964)
  the two profiles are of different devices: /device:TPU:18 before, /device:TPU:30 now
where the time goes in v4:
time: 189 us; the launch traced here: 188 us
  blocking collectives  90.2 us (48%)
  waiting for transfers between devices  47.6 us (25%)
  Pallas kernels  24.2 us (13%)
  starting transfers between devices  19.8 us (10%)
  local copies, waits for them, and re-layouts  5.71 us (3%)
    all_to_all x1, blocking collectives, exchange(): lax.all_to_all(rows.reshape(experts, chunk, width), 'expert', split_axis=...  90.2 us
    all_to_all x1, waiting for transfers between devices, exchange(): lax.all_to_all(rows.reshape(experts, chunk, width), 'expert', split_axis=...  29.6 us
    ppermute x3, waiting for transfers between devices, shards(): pieces.append(lax.ppermute(mine[step:step + 1], 'dp', hop))  14.6 us
    all_to_all x1, starting transfers between devices, exchange(): lax.all_to_all(rows.reshape(experts, chunk, width), 'expert', split_axis=...  9.28 us
    ppermute x3, starting transfers between devices, shards(): pieces.append(lax.ppermute(mine[step:step + 1], 'dp', hop))  8.62 us
    pallas_call x1, Pallas kernels, run_expert(): pl.pallas_call(expert_kernel, in_specs=[here, here, here, here], out_spec...  6.39 us
    pallas_call x2, Pallas kernels, weight_half(): pl.pallas_call(lambda *refs: weight_kernel(arrived is None, *refs), grid_...  6.31 us
    unnamed x20, local copies, waits for them, and re-layouts  5.6 us
  transfers between devices with their start and end apart: 5, of which 5 were waited for; matrix products, arithmetic and copies ran while one was open for 0% of the time, Pallas kernels for 6%

profile of v4, /device:TPU:30, one launch (start us, length us, event | category | flops | bytes accessed | tf_op | source)
XLA Modules:
  0.0 188.5 jit_solution(13504195608049114457)
XLA Ops:
  0.6 2.1 %pack.1 = bf16[1536,1024]{1,0:T(8,128)(2,1)S(1)} custom-call(s32[6,128]{1,0:T(8,128)} %bitcast.16, f32[6,128]{1,0:T(8,128)} %bitcast.18, bf16[128,1024]{1,0:T(8,128)(2,1)} %refs_2_.1, bf16[128,1024]{1,0:T(8,128)(2,1)} %refs_3_.1), custom_call_target="tpu_custom_call" | custom-call | flops 805306368 | bytes 3670016 | tf_op jit(solution)/shard_map/pack/pallas_call | solution.py:99
  2.8 0.0 copy-start.4
  2.8 0.0 copy-start.6
  2.8 0.0 copy-start.8
  2.8 90.2 %all_to_all.10 = bf16[64,24,1024]{2,1,0:T(8,128)(2,1)S(1)} all-to-all(bf16[64,24,1024]{2,1,0:T(8,128)(2,1)S(1)} %bitcast.12), channel_id=1, replica_groups={{0,33,2,35,4,37,6,39,8,41,10,43,12,45,14,47,16,49,18,51,20,53,22,55,24,..., dimensions={0} | all-to-all | bytes 6291456 | tf_op jit(solution)/shard_map/all_to_all | solution.py:433
  93.0 0.0 copy-done.8
  93.0 6.4 %expert.1 = bf16[1536,1024]{1,0:T(8,128)(2,1)} custom-call(bf16[1536,1024]{1,0:T(8,128)(2,1)S(1)} %bitcast.14, bf16[1024,512]{1,0:T(8,128)(2,1)S(1)} %bitcast.20, bf16[1024,512]{1,0:T(8,128)(2,1)S(1)} %bitcast.22, bf16[512,1024]{1,0:T(8,128)(2,1)S(1)} %bitcast.24), custom_call_target="tpu_custom_call" | custom-call | flops 4831838208 | bytes 11010048 | tf_op jit(solution)/shard_map/expert/pallas_call | solution.py:401
  99.4 9.3 %all-to-all-start.1 = ((bf16[64,24,1024]{2,1,0:T(8,128)(2,1)}), bf16[64,24,1024]{2,1,0:T(8,128)(2,1)S(1)}, u32[]{:S(2)}, u32[]{:S(2)}) async-start(bf16[64,24,1024]{2,1,0:T(8,128)(2,1)} %bitcast.26), calls=%async_computation.1 | async-start | bytes 6291456 | tf_op jit(solution)/shard_map/all_to_all | solution.py:433
  108.7 0.1 pad_add_fusion.1.refs_0_
  108.8 1.9 %copy-done.1 = bf16[64,24,1024]{2,1,0:T(8,128)(2,1)S(1)} copy-done((bf16[64,24,1024]{2,1,0:T(8,128)(2,1)S(1)}, bf16[64,24,1024]{2,1,0:T(8,128)(2,1)}, u32[]{:S(2)}) %copy-start.1) | copy-done | bytes 3145752
  110.7 1.2 copy-done.5
  111.9 1.2 copy-done.7
  113.1 1.2 copy-done.9
  114.4 2.9 %parts_again.1 = (bf16[768,1024]{1,0:T(8,128)(2,1)S(1)}, bf16[768,1024]{1,0:T(8,128)(2,1)S(1)}, bf16[768,1024]{1,0:T(8,128)(2,1)S(1)}, bf16[768,512]{1,0:T(8,128)(2,1)S(1)}) custom-call(bf16[1536,1024]{1,0:T(8,128)(2,1)S(1)} %bitcast.15, bf16[1024,512]{1,0:T(8,128)(2,1)S(1)} %bitcast.21, bf16[1024,512]{1,0:T(8,128)(2,1)S(1)} %bitcast.23, ...), custom_call_target="tpu_custom_call" | custom-call | flops 2415919104 | bytes 9437184 | tf_op jit(solution)/shard_map/parts_again/pallas_call | solution.py:327
  117.3 3.1 %weight_half.2 = bf16[4,128,1536]{2,1,0:T(8,128)(2,1)S(1)} custom-call(s32[2]{0:T(128)S(1)} %pad_add_fusion.1.refs_0_, bf16[768,1024]{1,0:T(8,128)(2,1)S(1)} %get-tuple-element.16.refs_1_, bf16[768,1024]{1,0:T(8,128)(2,1)S(1)} %get-tuple-element.17.refs_2_, bf16[768,1024]{1,0:T(8,128)(2,1)S(1)} %get-tuple-element.18.refs_3_, ...), custom_call_target="tpu_custom_call" | custom-call | flops 1207959552 | bytes 5505024 | tf_op jit(solution)/shard_map/weight_half/pallas_call | solution.py:231
  120.4 1.9 %collective-permute-start = (bf16[4,128,1536]{2,1,0:T(8,128)(2,1)S(1)}, bf16[4,128,1536]{2,1,0:T(8,128)(2,1)S(1)}, u32[]{:S(2)}, u32[]{:S(2)}) collective-permute-start(bf16[4,128,1536]{2,1,0:T(8,128)(2,1)S(1)} %weight_half.2), channel_id=1, source_target_pairs={{0,64},{64,0},{128,192},{192,128},{256,320},{320,256},{384,448},{4... | collective-permute-start | bytes 4718600 | tf_op jit(solution)/shard_map/ppermute | solution.py:449
  122.3 0.1 pad_add_fusion.refs_0_
  122.4 3.3 %collective-permute-done.refs_5_ = bf16[4,128,1536]{2,1,0:T(8,128)(2,1)S(1)} collective-permute-done((bf16[4,128,1536]{2,1,0:T(8,128)(2,1)S(1)}, bf16[4,128,1536]{2,1,0:T(8,128)(2,1)S(1)}, u32[]{:S(2)}, u32[]{:S(2)}) %collective-permute-start) | collective-permute-done | bytes 1572896 | tf_op jit(solution)/shard_map/ppermute | solution.py:449
  125.7 3.2 %weight_half.3 = bf16[4,128,1536]{2,1,0:T(8,128)(2,1)S(1)} custom-call(s32[2]{0:T(128)S(1)} %pad_add_fusion.refs_0_, bf16[768,1024]{1,0:T(8,128)(2,1)S(1)} %get-tuple-element.16.refs_1_, bf16[768,1024]{1,0:T(8,128)(2,1)S(1)} %get-tuple-element.17.refs_2_, bf16[768,1024]{1,0:T(8,128)(2,1)S(1)} %get-tuple-element.18.refs_3_, ...), custom_call_target="tpu_custom_call" | custom-call | flops 1207959552 | bytes 5505024 | tf_op jit(solution)/shard_map/weight_half/pallas_call | solution.py:231
  128.9 0.0 copy-start.2
  128.9 0.0 copy-start.3
  128.9 0.1 fusion
  129.0 2.4 %collective-permute-start.1 = (bf16[1,128,1536]{2,1,0:T(8,128)(2,1)S(1)}, bf16[1,128,1536]{2,1,0:T(8,128)(2,1)S(1)}, u32[]{:S(2)}, u32[]{:S(2)}) collective-permute-start(bf16[1,128,1536]{2,1,0:T(8,128)(2,1)S(1)} %get-tuple-element.25), channel_id=1, source_target_pairs={{0,128},{64,192},{128,256},{192,320},{256,384},{320,448},{384,0},{... | collective-permute-start | bytes 1179656 | tf_op jit(solution)/shard_map/ppermute | solution.py:454
  131.4 4.3 %collective-permute-start.2 = (bf16[1,128,1536]{2,1,0:T(8,128)(2,1)S(1)}, bf16[1,128,1536]{2,1,0:T(8,128)(2,1)S(1)}, u32[]{:S(2)}, u32[]{:S(2)}) collective-permute-start(bf16[1,128,1536]{2,1,0:T(8,128)(2,1)S(1)} %get-tuple-element.24), channel_id=1, source_target_pairs={{0,256},{64,320},{128,384},{192,448},{256,0},{320,64},{384,128},{4... | collective-permute-start | bytes 1179656 | tf_op jit(solution)/shard_map/ppermute | solution.py:454
  135.8 1.9 %collective-permute-start.3 = (bf16[1,128,1536]{2,1,0:T(8,128)(2,1)S(1)}, bf16[1,128,1536]{2,1,0:T(8,128)(2,1)S(1)}, u32[]{:S(2)}, u32[]{:S(2)}) collective-permute-start(bf16[1,128,1536]{2,1,0:T(8,128)(2,1)S(1)} %get-tuple-element.23), channel_id=1, source_target_pairs={{0,384},{64,448},{128,0},{192,64},{256,128},{320,192},{384,256},{4... | collective-permute-start | bytes 1179656 | tf_op jit(solution)/shard_map/ppermute | solution.py:454
  137.7 1.8 plan.1.plan_hbm
  139.5 3.4 %collective-permute-done.1.refs_1_ = bf16[1,128,1536]{2,1,0:T(8,128)(2,1)S(1)} collective-permute-done((bf16[1,128,1536]{2,1,0:T(8,128)(2,1)S(1)}, bf16[1,128,1536]{2,1,0:T(8,128)(2,1)S(1)}, u32[]{:S(2)}, u32[]{:S(2)}) %collective-permute-start.1) | collective-permute-done | bytes 393248 | tf_op jit(solution)/shard_map/ppermute | solution.py:454
  142.9 4.0 %collective-permute-done.2.refs_2_ = bf16[1,128,1536]{2,1,0:T(8,128)(2,1)S(1)} collective-permute-done((bf16[1,128,1536]{2,1,0:T(8,128)(2,1)S(1)}, bf16[1,128,1536]{2,1,0:T(8,128)(2,1)S(1)}, u32[]{:S(2)}, u32[]{:S(2)}) %collective-permute-start.2) | collective-permute-done | bytes 393248 | tf_op jit(solution)/shard_map/ppermute | solution.py:454
  146.9 7.3 %collective-permute-done.3.refs_3_ = bf16[1,128,1536]{2,1,0:T(8,128)(2,1)S(1)} collective-permute-done((bf16[1,128,1536]{2,1,0:T(8,128)(2,1)S(1)}, bf16[1,128,1536]{2,1,0:T(8,128)(2,1)S(1)}, u32[]{:S(2)}, u32[]{:S(2)}) %collective-permute-start.3) | collective-permute-done | bytes 393248 | tf_op jit(solution)/shard_map/ppermute | solution.py:454
  154.1 1.0 finish.1
  155.2 29.6 %all-to-all-done.1 = bf16[64,24,1024]{2,1,0:T(8,128)(2,1)S(1)} async-done(((bf16[64,24,1024]{2,1,0:T(8,128)(2,1)}), bf16[64,24,1024]{2,1,0:T(8,128)(2,1)S(1)}, u32[]{:S(2)}, u32[]{:S(2)}) %all-to-all-start.1) | async-done | bytes 3145760 | tf_op jit(solution)/shard_map/all_to_all | solution.py:433
  184.8 3.7 %unpack.1 = (bf16[128,1024]{1,0:T(8,128)(2,1)}, bf16[128,1024]{1,0:T(8,128)(2,1)}) custom-call(bf16[1536,384]{1,0:T(8,128)(2,1)} %plan.1.plan_hbm, bf16[1536,1024]{1,0:T(8,128)(2,1)S(1)} %bitcast.13), custom_call_target="tpu_custom_call" | custom-call | flops 1207959552 | bytes 4456448 | tf_op jit(solution)/shard_map/unpack/pallas_call | solution.py:186
  (10 shorter events, 0.0 us)
Async XLA Ops:
  2.8 90.2 %copy-start.4 = (bf16[1,1024,512]{2,1,0:T(8,128)(2,1)S(1)}, bf16[1,1024,512]{2,1,0:T(8,128)(2,1)}, u32[]{:S(2)}) copy-start(bf16[1,1024,512]{2,1,0:T(8,128)(2,1)} %param.10) | copy-start | bytes 3145732
  2.8 90.2 %copy-start.6 = (bf16[1,1024,512]{2,1,0:T(8,128)(2,1)S(1)}, bf16[1,1024,512]{2,1,0:T(8,128)(2,1)}, u32[]{:S(2)}) copy-start(bf16[1,1024,512]{2,1,0:T(8,128)(2,1)} %param.11) | copy-start | bytes 3145732
  2.8 90.2 %copy-start.8 = (bf16[1,512,1024]{2,1,0:T(8,128)(2,1)S(1)}, bf16[1,512,1024]{2,1,0:T(8,128)(2,1)}, u32[]{:S(2)}) copy-start(bf16[1,512,1024]{2,1,0:T(8,128)(2,1)} %param.12) | copy-start | bytes 3145732
  93.0 6.4 %copy-start = (bf16[64,24,1024]{2,1,0:T(8,128)(2,1)}, bf16[64,24,1024]{2,1,0:T(8,128)(2,1)S(1)}, u32[]{:S(2)}) copy-start(bf16[64,24,1024]{2,1,0:T(8,128)(2,1)S(1)} %all_to_all.10) | copy-start | bytes 9437188
  99.4 85.4 %all-to-all-start.1 = ((bf16[64,24,1024]{2,1,0:T(8,128)(2,1)}), bf16[64,24,1024]{2,1,0:T(8,128)(2,1)S(1)}, u32[]{:S(2)}, u32[]{:S(2)}) async-start(bf16[64,24,1024]{2,1,0:T(8,128)(2,1)} %bitcast.26), calls=%async_computation.1 | async-start | bytes 6291456 | tf_op jit(solution)/shard_map/all_to_all | solution.py:433
  108.8 1.9 %copy-start.1 = (bf16[64,24,1024]{2,1,0:T(8,128)(2,1)S(1)}, bf16[64,24,1024]{2,1,0:T(8,128)(2,1)}, u32[]{:S(2)}) copy-start(bf16[64,24,1024]{2,1,0:T(8,128)(2,1)} %copy-done) | copy-start | bytes 9437188
  110.7 1.2 copy-start.5
  111.9 1.2 copy-start.7
  113.1 1.2 copy-start.9
  120.4 5.3 %collective-permute-start = (bf16[4,128,1536]{2,1,0:T(8,128)(2,1)S(1)}, bf16[4,128,1536]{2,1,0:T(8,128)(2,1)S(1)}, u32[]{:S(2)}, u32[]{:S(2)}) collective-permute-start(bf16[4,128,1536]{2,1,0:T(8,128)(2,1)S(1)} %weight_half.2), channel_id=1, source_target_pairs={{0,64},{64,0},{128,192},{192,128},{256,320},{320,256},{384,448},{4... | collective-permute-start | bytes 4718600 | tf_op jit(solution)/shard_map/ppermute | solution.py:449
  128.9 8.8 %copy-start.2 = (s32[128,6]{0,1:T(8,128)S(1)}, s32[128,6]{0,1:T(8,128)}, u32[]{:S(2)}) copy-start(s32[128,6]{0,1:T(8,128)} %param.8) | copy-start | bytes 9220
  128.9 8.8 %copy-start.3 = (f32[128,6]{0,1:T(8,128)S(1)}, f32[128,6]{0,1:T(8,128)}, u32[]{:S(2)}) copy-start(f32[128,6]{0,1:T(8,128)} %param.9) | copy-start | bytes 9220
  129.0 13.9 %collective-permute-start.1 = (bf16[1,128,1536]{2,1,0:T(8,128)(2,1)S(1)}, bf16[1,128,1536]{2,1,0:T(8,128)(2,1)S(1)}, u32[]{:S(2)}, u32[]{:S(2)}) collective-permute-start(bf16[1,128,1536]{2,1,0:T(8,128)(2,1)S(1)} %get-tuple-element.25), channel_id=1, source_target_pairs={{0,128},{64,192},{128,256},{192,320},{256,384},{320,448},{384,0},{... | collective-permute-start | bytes 1179656 | tf_op jit(solution)/shard_map/ppermute | solution.py:454
  131.4 15.4 %collective-permute-start.2 = (bf16[1,128,1536]{2,1,0:T(8,128)(2,1)S(1)}, bf16[1,128,1536]{2,1,0:T(8,128)(2,1)S(1)}, u32[]{:S(2)}, u32[]{:S(2)}) collective-permute-start(bf16[1,128,1536]{2,1,0:T(8,128)(2,1)S(1)} %get-tuple-element.24), channel_id=1, source_target_pairs={{0,256},{64,320},{128,384},{192,448},{256,0},{320,64},{384,128},{4... | collective-permute-start | bytes 1179656 | tf_op jit(solution)/shard_map/ppermute | solution.py:454
  135.8 18.4 %collective-permute-start.3 = (bf16[1,128,1536]{2,1,0:T(8,128)(2,1)S(1)}, bf16[1,128,1536]{2,1,0:T(8,128)(2,1)S(1)}, u32[]{:S(2)}, u32[]{:S(2)}) collective-permute-start(bf16[1,128,1536]{2,1,0:T(8,128)(2,1)S(1)} %get-tuple-element.23), channel_id=1, source_target_pairs={{0,384},{64,448},{128,0},{192,64},{256,128},{320,192},{384,256},{4... | collective-permute-start | bytes 1179656 | tf_op jit(solution)/shard_map/ppermute | solution.py:454
